TPU v7x, 32 devices: a whole 2x2x4 slice. The times are simulated.
32 devices in a mesh: seq: 8 (over z, y), head: 4 (over x, core).
Axes of the slice: x: 2, y: 2, z: 4, core: 2. Of those that a mesh axis runs over, the one named last changes fastest.
Arguments:
- frames: bfloat16 [24576, 8192], P('seq', 'head'), may hold values from -6 to 6
- state_proj: bfloat16 [256, 24576], P('head', 'seq'), as said below
- log_decay: float32 [128, 24576], P('head', 'seq'), may hold values from -0.7 to 0
- skip_gain: float32 [128], P('head'), may hold values from 0.1 to 1.9
- group_pos: int32 [96], P('seq'), may hold values from 0 to 95, as said below
Outputs:
- mixed: bfloat16 [24576, 8192], P('seq', 'head')
Inputs may be any that keep to these rules, and one draw needn't show every extreme that they name: `group_pos`: device d of seq holds in its 12 slots the groups of sequence positions d * 12 to (d + 1) * 12 - 1, each once, in an order drawn from the seed. `state_proj`: entries lie within 5 times their scale, which is the inverse fourth root of 393216.
All inputs are finite; a program needn't handle non-finite values.
Results may differ from a plain program's by a relative error of at most 0.0053.
Values may be sent and summed in bfloat16 or wider, within the bound.
A program may use at most 128 MiB of HBM per device.

v0:
```python
import jax
import jax.numpy as jnp
from jax import lax
from jax.sharding import PartitionSpec as P

HEAD_DIM = 64
STATE = 128
GROUP = 256


def prefix_matrix(length):
    step_ids = jnp.arange(length)
    return (step_ids[:, None] <= step_ids[None, :]).astype(jnp.float32)


def group_terms(inputs, group_in, natlog_speeds, upper):
    running = jnp.dot(natlog_speeds, upper, precision=lax.Precision.HIGHEST)
    input_map = group_in[:STATE]
    output_map = group_in[STATE:]
    coupling = lax.dot_general(
        output_map, input_map, (((0,), (0,)), ((), ())), preferred_element_type=jnp.float32
    )
    step_ids = jnp.arange(running.shape[1])
    causal = (step_ids[:, None] >= step_ids[None, :])[None]
    log_gap = running[:, :, None] - running[:, None, :]
    decay_table = jnp.where(causal, jnp.exp(jnp.where(causal, log_gap, 0.0)), 0.0)
    weights = (coupling[None] * decay_table).astype(jnp.bfloat16)
    within = jnp.einsum("hts,shp->thp", weights, inputs, preferred_element_type=jnp.float32)
    group_log = running[:, -1]
    carried = (inputs * jnp.exp(group_log[:, None] - running).T[:, :, None]).astype(jnp.bfloat16)
    summary = jnp.einsum("shp,ns->hpn", carried, input_map, preferred_element_type=jnp.float32)
    return (within, summary, running)


def shards(frames, state_proj, log_decay, skip_gain, group_pos):
    whole_proj = lax.all_gather(state_proj, "head", axis=0, tiled=True)
    group_count = group_pos.shape[0]
    heads_here = skip_gain.shape[0]
    ordinal_place = group_pos - lax.axis_index("seq") * group_count
    slot_ids = jnp.arange(group_count, dtype=jnp.int32)
    inverse = jnp.sum(
        jnp.where(ordinal_place[:, None] == slot_ids[None, :], slot_ids[:, None], 0), axis=0
    )
    inputs = frames.reshape(group_count, GROUP, heads_here, HEAD_DIM)[inverse]
    projections = whole_proj.reshape(2 * STATE, group_count, GROUP).transpose(1, 0, 2)[inverse]
    natlog_speeds = log_decay.reshape(heads_here, group_count, GROUP).transpose(1, 0, 2)[inverse]
    upper = prefix_matrix(GROUP)
    within, summary, running = lax.map(
        lambda group_item: group_terms(group_item[0], group_item[1], group_item[2], upper),
        (inputs, projections, natlog_speeds),
    )
    group_log = running[:, :, -1]

    def advance(carry_state, group_item):
        return (jnp.exp(group_item[1])[:, None, None] * carry_state + group_item[0], carry_state)

    empty_state = jnp.zeros((heads_here, HEAD_DIM, STATE), jnp.float32)
    local_end, segment_prior = lax.scan(advance, empty_state, (summary, group_log))
    total_log = jnp.sum(group_log, axis=0)
    before_log = jnp.cumsum(group_log, axis=0) - group_log
    linear_stop = local_end.reshape(1, heads_here, HEAD_DIM * STATE)
    slices = lax.all_to_all(linear_stop, "seq", split_axis=2, concat_axis=0, tiled=True)
    shard_logs = lax.all_gather(total_log[None], "seq", axis=0, tiled=True)
    through = jnp.cumsum(shard_logs, axis=0)
    before_shard = through - shard_logs
    shard_ids = jnp.arange(shard_logs.shape[0])
    lower = (shard_ids[:, None] > shard_ids[None, :])[:, :, None]
    log_span = before_shard[:, None, :] - through[None, :, :]
    factors = jnp.where(lower, jnp.exp(jnp.where(lower, log_span, 0.0)), 0.0)
    entering = jnp.einsum("kjh,jhe->khe", factors, slices, precision=lax.Precision.HIGHEST)
    returned = lax.all_to_all(entering, "seq", split_axis=0, concat_axis=2, tiled=True)
    carry_in = returned.reshape(heads_here, HEAD_DIM, STATE)
    held_state = (jnp.exp(before_log)[:, :, None, None] * carry_in[None] + segment_prior).astype(
        jnp.bfloat16
    )
    across_shards = jnp.einsum(
        "chpn,cnt->cthp", held_state, projections[:, STATE:], preferred_element_type=jnp.float32
    )
    across_shards = across_shards * jnp.exp(running).transpose(0, 2, 1)[:, :, :, None]
    output = (
        within + across_shards + skip_gain[None, None, :, None] * inputs.astype(jnp.float32)
    ).astype(jnp.bfloat16)
    return output.reshape(group_count * GROUP, heads_here * HEAD_DIM)


def solution(mesh):
    return jax.shard_map(
        shards,
        mesh=mesh,
        in_specs=(P("seq", "head"), P("head", "seq"), P("head", "seq"), P("head"), P("seq")),
        out_specs=P("seq", "head"),
        check_vma=False,
    )
```

profile of v0, /device:TPU:24, one launch (start us, length us, event | category | flops | bytes accessed | tf_op | source)
XLA Modules:
  0.0 471.4 jit_solution(13330650402835290313)
XLA Ops:
  7.3 36.2 %reshape.122 = bf16[12,256,32,64]{3,2,1,0:T(8,128)(2,1)} reshape(bf16[3072,2048]{1,0:T(8,128)(2,1)} %param.9) | data formatting | bytes 25165824 | tf_op jit(solution)/shard_map/reshape | solution.py:44
  43.5 28.5 %copy.45 = bf16[12,256,32,64]{1,3,2,0:T(8,128)(2,1)} copy(bf16[12,256,32,64]{3,2,1,0:T(8,128)(2,1)} %reshape.122) | data formatting | bytes 25165824 | tf_op jit(solution)/shard_map/reshape | solution.py:44
  72.2 10.6 %gather_fusion = bf16[12,256,32,64]{1,3,2,0:T(8,128)(2,1)} fusion(bf16[12,256,32,64]{1,3,2,0:T(8,128)(2,1)} %copy.45, s32[1024]{0:T(1024)S(1)} %pad_clamp_fusion), kind=kCustom, calls=%fused_computation | custom fusion | bytes 25165872 | tf_op jit(solution)/shard_map/gather | solution.py:44
  89.5 6.4 %broadcast.45.clone = f32[12,32,64,128]{3,2,1,0:T(8,128)} broadcast(f32[]{:T(128)} %constant.35.clone.1), dimensions={} | broadcast | bytes 12582916 | tf_op jit(solution)/shard_map/broadcast.3
  95.8 104.7 %while.28 = (s32[]{:T(128)}, f32[12,256,32,64]{1,3,2,0:T(8,128)}, f32[12,32,64,128]{3,2,1,0:T(8,128)}, f32[12,32,256]{2,1,0:T(8,128)S(1)}, bf16[12,256,32,64]{1,...) while((s32[]{:T(128)}, f32[12,256,32,64]{1,3,2,0:T(8,128)}, ...), condition=%wide.region_2.3_spmd.clone, body=%wide.region_1.2_spmd.clone.sunk | while | flops 456859648 | bytes 6362101 | solution.py:48
  100.0 4.6 bitcast_dynamic-update-slice_fusion.7
  108.8 4.5 bitcast_dynamic-update-slice_fusion.7
  117.5 4.6 bitcast_dynamic-update-slice_fusion.7
  126.2 4.5 bitcast_dynamic-update-slice_fusion.7
  135.0 4.5 bitcast_dynamic-update-slice_fusion.7
  143.7 4.5 bitcast_dynamic-update-slice_fusion.7
  152.4 4.5 bitcast_dynamic-update-slice_fusion.7
  161.1 4.6 bitcast_dynamic-update-slice_fusion.7
  169.8 4.6 bitcast_dynamic-update-slice_fusion.7
  178.6 4.5 bitcast_dynamic-update-slice_fusion.7
  187.3 4.6 bitcast_dynamic-update-slice_fusion.7
  196.0 4.5 bitcast_dynamic-update-slice_fusion.7
  203.7 6.1 %broadcast.45 = f32[12,32,64,128]{3,2,1,0:T(8,128)} broadcast(f32[]{:T(128)} %constant.35.clone.1), dimensions={} | broadcast | bytes 12582916 | tf_op jit(solution)/shard_map/broadcast.3
  209.8 30.0 %while.29 = (s32[]{:T(128)}, f32[32,64,128]{2,1,0:T(8,128)S(1)}, f32[12,32,64,128]{3,2,1,0:T(8,128)}, f32[12,32]{1,0:T(8,128)S(1)}, f32[12,32,64,128]{3,2,1,0:T(8,128)}, /*index=5*/s32[]{:T(128)}, s32[]{:T(128)}) while((s32[]{:T(128)}, f32[32,64,128]{2,1,0:T(8,128)S(1)}, f32[12,32,64,128]{3,2,1,0:T(8,128)}, ...), condition=%wide.region_5.6_spmd.clone, body=%wide.region_4.5_spmd.clone.sunk | while | flops 1048579 | bytes 5243872 | solution.py:58
  239.8 2.7 copy.50
  243.0 38.6 %reduce.3 = f32[8192,32]{1,0:T(8,128)} reduce(f32[8192,1,32]{2,1,0:T(1,128)} %bitcast.108, f32[]{:T(128)} %broadcast.68), dimensions={1}, to_apply=%bitcast.75.reduce_sub_computation | reduce | bytes 2097156
  281.5 4.8 %reshape.125 = f32[8,1,32768]{2,1,0:T(1,128)} reshape(f32[8192,32]{1,0:T(8,128)} %reduce.3) | data formatting | bytes 2097152
  286.4 6.2 %all-to-all-start = ((f32[8,1,32768]{2,1,0:T(1,128)}), f32[8,1,32768]{2,1,0:T(1,128)}, u32[]{:S(2)}, u32[]{:S(2)}) async-start(f32[8,1,32768]{2,1,0:T(1,128)} %reshape.125), calls=%async_computation | async-start | bytes 2097152 | tf_op jit(solution)/shard_map/all_to_all | solution.py:62
  294.0 31.3 %all-reduce = f32[256]{0:T(256)S(1)} all-reduce(f32[256]{0:T(256)S(1)} %dynamic-update-slice), channel_id=2, replica_groups=mesh['seq'=8,'head'=4] {'seq'}, use_global_device_ids=true, to_apply=%add | all-reduce | flops 256 | bytes 2048
  325.5 4.3 reduce.4
  329.8 8.8 %reshape.126 = f32[8192,1,32]{2,1,0:T(1,128)} reshape(f32[8,32768]{1,0:T(8,128)S(1)} %reduce.4) | data formatting | bytes 2097152
  338.6 3.0 copy.61
  344.3 5.1 %all-to-all-start.1 = ((f32[8,32,1024]{2,1,0:T(8,128)}), f32[8,32,1024]{2,1,0:T(8,128)S(1)}, u32[]{:S(2)}, u32[]{:S(2)}) async-start(f32[8,32,1024]{2,1,0:T(8,128)} %copy.54), calls=%async_computation.1 | async-start | bytes 2097152 | tf_op jit(solution)/shard_map/all_to_all | solution.py:71
  350.2 20.0 %all-to-all-done.1 = f32[8,32,1024]{2,1,0:T(8,128)S(1)} async-done(((f32[8,32,1024]{2,1,0:T(8,128)}), f32[8,32,1024]{2,1,0:T(8,128)S(1)}, u32[]{:S(2)}, u32[]{:S(2)}) %all-to-all-start.1) | async-done | bytes 1048608 | tf_op jit(solution)/shard_map/all_to_all | solution.py:71
  373.2 21.8 %add_convert_fusion = bf16[12,256,32,64]{1,3,2,0:T(8,128)(2,1)} fusion(bf16[12,256,32,64]{1,3,2,0:T(8,128)(2,1)} %get-tuple-element.274, f32[12,256,32,64]{1,3,2,0:T(8,128)} %get-tuple-element.77, f32[32]{0:T(128)S(1)} %copy-done.1, f32[12,256,32]{1,2,0:T(8,128)S(1)} %exponential_bitcast_fusion.1, f32[12,32,64,128]{3,2,1,0:T(8,128)} %get-tuple-element.81, ...), kind=kOutput, calls=%fused_computation.45 | convolution fusion | flops 1657798656 | bytes 65151488 | tf_op jit(solution)/shard_map/chpn,cnt->cthp/dot_general | solution.py:76
  395.0 34.9 %copy.62 = bf16[12,256,32,64]{3,2,1,0:T(8,128)(2,1)} copy(bf16[12,256,32,64]{1,3,2,0:T(8,128)(2,1)} %add_convert_fusion) | data formatting | bytes 25165824 | tf_op jit(solution)/shard_map/reshape | solution.py:83
  429.9 34.7 %reshape.123 = bf16[3072,2048]{1,0:T(8,128)(2,1)} reshape(bf16[12,256,32,64]{3,2,1,0:T(8,128)(2,1)} %copy.62) | data formatting | bytes 25165824 | tf_op jit(solution)/shard_map/reshape | solution.py:83
  (151 shorter events, 98.0 us)
Async XLA Ops:
  6.5 77.6 %all-gather.3.cloned.1.call-start = ((), (), s32[]{:S(2)}) async-start(), calls=%async_computation.2 | async-start | bytes 1966080 | tf_op jit(solution)/shard_map/all_gather | solution.py:36
  43.5 28.5 %copy-start = (f32[32,3072]{1,0:T(8,128)S(1)}, f32[32,3072]{1,0:T(8,128)}, u32[]{:S(2)}) copy-start(f32[32,3072]{1,0:T(8,128)} %param.11) | copy-start | bytes 1179652
  43.5 28.5 %copy-start.2 = (s32[12]{0:T(128)S(1)}, s32[12]{0:T(128)}, u32[]{:S(2)}) copy-start(s32[12]{0:T(128)} %param.13) | copy-start | bytes 148
  239.8 52.8 %copy-start.3 = (u32[32]{0:T(128)S(1)}, u32[32]{0:T(128)}, u32[]{:S(2)}) copy-start(u32[32]{0:T(128)} %constant.56) | copy-start | bytes 388
  286.4 86.8 %copy-start.1 = (f32[32]{0:T(128)S(1)}, f32[32]{0:T(128)}, u32[]{:S(2)}) copy-start(f32[32]{0:T(128)} %param.12) | copy-start | bytes 388
  286.4 39.1 %all-to-all-start = ((f32[8,1,32768]{2,1,0:T(1,128)}), f32[8,1,32768]{2,1,0:T(1,128)}, u32[]{:S(2)}, u32[]{:S(2)}) async-start(f32[8,1,32768]{2,1,0:T(1,128)} %reshape.125), calls=%async_computation | async-start | bytes 2097152 | tf_op jit(solution)/shard_map/all_to_all | solution.py:62
  344.3 25.9 %all-to-all-start.1 = ((f32[8,32,1024]{2,1,0:T(8,128)}), f32[8,32,1024]{2,1,0:T(8,128)S(1)}, u32[]{:S(2)}, u32[]{:S(2)}) async-start(f32[8,32,1024]{2,1,0:T(8,128)} %copy.54), calls=%async_computation.1 | async-start | bytes 2097152 | tf_op jit(solution)/shard_map/all_to_all | solution.py:71
Sparse Core Ops, SparseCore 0:
  8.9 20.6 all-gather.2
where the time goes:
time: 481 us; the launch traced here: 471 us
  local copies, waits for them, and re-layouts  194 us (40%)
  matrix products  124 us (26%)
  other arithmetic  75.4 us (16%)
  blocking collectives  31.3 us (7%)
  waiting for transfers between devices  20.7 us (4%)
  between operations  14.1 us (3%)
  starting transfers between devices  11.3 us (2%)
    reshape x2, local copies, waits for them, and re-layouts, shards(): return output.reshape(group_count * GROUP, heads_here * HEAD_DIM)  69.6 us
    reshape x2, local copies, waits for them, and re-layouts, shards(): inputs = frames.reshape(group_count, GROUP, heads_here, HEAD_DIM)[inverse]  64.7 us
    dot_general x12, matrix products, group_terms(): jnp.einsum('hts,shp->thp', weights, inputs, preferred_element_type=jnp.fl...  54.7 us
    unnamed x2, other arithmetic  38.6 us
    dot_general x12, matrix products, group_terms(): jnp.einsum('shp,ns->hpn', carried, input_map, preferred_element_type=jnp....  31.8 us
    unnamed x1, blocking collectives  31.3 us
    dot_general x1, matrix products, shards(): jnp.einsum('chpn,cnt->cthp', held_state, projections[:, STATE:], preferre...  21.8 us
    all_to_all x1, waiting for transfers between devices, shards(): lax.all_to_all(entering, 'seq', split_axis=0, concat_axis=2, tiled=True)  20 us
  transfers between devices with their start and end apart: 3, of which 1 were waited for; matrix products, arithmetic and copies ran while one was open for 17% of the time, Pallas kernels for 0%

commit v1 on v0

v1 whole, which is shorter than its diff:
```python
import functools

import jax
import jax.numpy as jnp
from jax import lax
from jax.experimental import pallas as pl
from jax.experimental.pallas import tpu as pltpu
from jax.sharding import PartitionSpec as P

HEAD_DIM = 64
STATE = 128
GROUP = 256
CHUNK = 128
TILE = 256
VMEM_BYTES = 48 * 1024 * 1024


def spread_matrix(heads, columns):
    rows = lax.broadcasted_iota(jnp.int32, (2 * heads, columns), 0) % heads
    owner = lax.broadcasted_iota(jnp.int32, (2 * heads, columns), 1) // HEAD_DIM
    return (rows == owner).astype(jnp.float32).astype(jnp.bfloat16)


def lower_matrix(length):
    rows = lax.broadcasted_iota(jnp.int32, (length, length), 0)
    columns = lax.broadcasted_iota(jnp.int32, (length, length), 1)
    return rows >= columns


def running_sums(logs, lower):
    twice = jnp.concatenate([logs, logs], axis=0)
    high = twice.astype(jnp.bfloat16)
    rest = twice - high.astype(jnp.float32)
    middle = rest.astype(jnp.bfloat16)
    low = (rest - middle.astype(jnp.float32)).astype(jnp.bfloat16)
    total = None
    for term in (low, middle, high):
        part = lax.dot_general(
            lower, term, (((1,), (1,)), ((), ())), preferred_element_type=jnp.float32
        )
        total = part if total is None else total + part
    return total


def two_terms(values, heads):
    high = values.astype(jnp.bfloat16).astype(jnp.float32)
    lanes = lax.broadcasted_iota(jnp.int32, values.shape, 1)
    return jnp.where(lanes < heads, high, values - high).astype(jnp.bfloat16)


def summary_kernel(x_ref, proj_ref, log_ref, after_ref, out_ref, acc_ref, spread_ref):
    step = pl.program_id(0)
    heads = log_ref.shape[0]
    columns = x_ref.shape[1]

    @pl.when(step == 0)
    def _():
        acc_ref[...] = jnp.zeros_like(acc_ref)
        spread_ref[...] = spread_matrix(heads, columns)

    lower = lower_matrix(GROUP).astype(jnp.float32).astype(jnp.bfloat16)
    running = running_sums(log_ref[...], lower)
    decay = two_terms(jnp.exp(after_ref[0] - running), heads)
    for start in range(0, columns, TILE):
        tile = slice(start, start + TILE)
        wide = jnp.dot(decay, spread_ref[:, tile], preferred_element_type=jnp.float32)
        carried = (x_ref[:, tile].astype(jnp.float32) * wide).astype(jnp.bfloat16)
        acc_ref[:, tile] += jnp.dot(proj_ref[...], carried, preferred_element_type=jnp.float32)

    @pl.when(step == pl.num_programs(0) - 1)
    def _():
        out_ref[...] = acc_ref[...].astype(out_ref.dtype)


def summarise(frames, proj, logs, after):
    frame_count, columns = frames.shape
    heads = logs.shape[0]
    groups = frame_count // GROUP
    return pl.pallas_call(
        summary_kernel,
        grid=(groups,),
        in_specs=[
            pl.BlockSpec((GROUP, columns), lambda i: (i, 0)),
            pl.BlockSpec((STATE, GROUP), lambda i: (0, i)),
            pl.BlockSpec((heads, GROUP), lambda i: (0, i)),
            pl.BlockSpec((1, 1, 2 * heads), lambda i: (i, 0, 0)),
        ],
        out_specs=pl.BlockSpec((STATE, columns), lambda i: (0, 0)),
        out_shape=jax.ShapeDtypeStruct((STATE, columns), jnp.bfloat16),
        scratch_shapes=[
            pltpu.VMEM((STATE, columns), jnp.float32),
            pltpu.VMEM((2 * heads, columns), jnp.bfloat16),
        ],
        compiler_params=pltpu.CompilerParams(vmem_limit_bytes=VMEM_BYTES),
        cost_estimate=pl.CostEstimate(
            flops=4 * frame_count * columns * STATE,
            bytes_accessed=2 * frame_count * columns,
            transcendentals=frame_count * heads,
        ),
        name="summary",
    )(frames, proj, logs, after)


def mix_kernel(
    slot_ref, x_ref, proj_ref, log_ref, skip_ref, enter_ref, out_ref, state_ref, spread_ref, both_ref
):
    step = pl.program_id(0)
    heads = log_ref.shape[0]
    columns = x_ref.shape[1]

    @pl.when(step == 0)
    def _():
        state_ref[...] = enter_ref[...].astype(jnp.float32)
        spread_ref[...] = spread_matrix(heads, columns)

    causal = lower_matrix(CHUNK)
    lower = causal.astype(jnp.float32).astype(jnp.bfloat16)
    half = CHUNK // 2
    for first in range(0, GROUP, CHUNK):
        rows = slice(first, first + CHUNK)
        running = running_sums(log_ref[:, rows], lower)
        middle = running[half - 1 : half]
        last = running[CHUNK - 1 : CHUNK]
        extra = lax.broadcasted_iota(jnp.int32, (16, 2 * heads), 0)
        exponents = jnp.concatenate(
            [middle - running, running - middle, jnp.where(extra == 0, middle, last - middle)], axis=0
        )
        decay = two_terms(jnp.exp(exponents), heads)
        input_map = proj_ref[:STATE, rows]
        output_map = proj_ref[STATE:, rows].astype(jnp.float32).T.astype(jnp.bfloat16)
        coupling = jnp.dot(output_map, input_map, preferred_element_type=jnp.float32)
        coupling = jnp.where(causal, coupling, 0.0).astype(jnp.bfloat16)
        left = jnp.concatenate([coupling, output_map], axis=1)
        for start in range(0, columns, TILE):
            tile = slice(start, start + TILE)
            wide = jnp.dot(decay, spread_ref[:, tile], preferred_element_type=jnp.float32)
            x = x_ref[rows, tile].astype(jnp.float32)
            scaled = (x * wide[:CHUNK]).astype(jnp.bfloat16)
            prior = state_ref[:, tile] * wide[2 * CHUNK : 2 * CHUNK + 1]
            both_ref[:CHUNK, tile] = scaled
            both_ref[CHUNK:, tile] = prior.astype(jnp.bfloat16)
            mixed = jnp.dot(left, both_ref[:, tile], preferred_element_type=jnp.float32)
            out_ref[rows, tile] = (
                mixed * wide[CHUNK : 2 * CHUNK] + skip_ref[:, tile] * x
            ).astype(out_ref.dtype)
            update = jnp.dot(input_map, scaled, preferred_element_type=jnp.float32)
            state_ref[:, tile] = (prior + update) * wide[2 * CHUNK + 1 : 2 * CHUNK + 2]


def mix(slots, frames, proj, logs, skip, entering):
    frame_count, columns = frames.shape
    heads = logs.shape[0]
    groups = frame_count // GROUP
    grid_spec = pltpu.PrefetchScalarGridSpec(
        num_scalar_prefetch=1,
        grid=(groups,),
        in_specs=[
            pl.BlockSpec((GROUP, columns), lambda i, slot: (slot[i], 0)),
            pl.BlockSpec((2 * STATE, GROUP), lambda i, slot: (0, slot[i])),
            pl.BlockSpec((heads, GROUP), lambda i, slot: (0, slot[i])),
            pl.BlockSpec((1, columns), lambda i, slot: (0, 0)),
            pl.BlockSpec((STATE, columns), lambda i, slot: (0, 0)),
        ],
        out_specs=pl.BlockSpec((GROUP, columns), lambda i, slot: (i, 0)),
        scratch_shapes=[
            pltpu.VMEM((STATE, columns), jnp.float32),
            pltpu.VMEM((2 * heads, columns), jnp.bfloat16),
            pltpu.VMEM((2 * STATE, columns), jnp.bfloat16),
        ],
    )
    return pl.pallas_call(
        mix_kernel,
        grid_spec=grid_spec,
        out_shape=jax.ShapeDtypeStruct((frame_count, columns), jnp.bfloat16),
        compiler_params=pltpu.CompilerParams(vmem_limit_bytes=VMEM_BYTES),
        cost_estimate=pl.CostEstimate(
            flops=8 * frame_count * columns * STATE,
            bytes_accessed=4 * frame_count * columns,
            transcendentals=2 * frame_count * heads,
        ),
        name="mix",
    )(slots, frames, proj, logs, skip, entering)


def per_channel(values):
    return jnp.repeat(values, HEAD_DIM, axis=-1)


def enter_states(summary, total_log, shard_count):
    columns = summary.shape[1]
    slices = lax.all_to_all(summary[None], "seq", split_axis=1, concat_axis=0, tiled=True)
    shard_logs = lax.all_gather(total_log[None], "seq", axis=0, tiled=True)
    through = jnp.cumsum(shard_logs, axis=0)
    before_shard = through - shard_logs
    ids = jnp.arange(shard_count)
    earlier = (ids[:, None] > ids[None, :])[:, :, None]
    span = before_shard[:, None, :] - through[None, :, :]
    factors = per_channel(jnp.where(earlier, jnp.exp(jnp.where(earlier, span, 0.0)), 0.0))
    entering = jnp.sum(factors[:, :, None, :] * slices.astype(jnp.float32)[None], axis=1)
    entering = entering.astype(jnp.bfloat16)
    returned = lax.all_to_all(entering, "seq", split_axis=0, concat_axis=1, tiled=True)
    return returned.reshape(STATE, columns)


def shards(shard_count, frames, state_proj, log_decay, skip_gain, group_pos):
    proj = lax.all_gather(state_proj, "head", axis=0, tiled=True)
    groups = group_pos.shape[0]
    heads = skip_gain.shape[0]
    place = group_pos - lax.axis_index("seq") * groups
    slot_ids = jnp.arange(groups, dtype=jnp.int32)
    slots = jnp.sum(jnp.where(place[:, None] == slot_ids[None, :], slot_ids[:, None], 0), axis=0)
    group_log = jnp.sum(log_decay.reshape(heads, groups, GROUP), axis=2)
    onward = group_pos[None, :] >= group_pos[:, None]
    after = jnp.sum(jnp.where(onward[:, None, :], group_log[None], 0.0), axis=2)
    total_log = jnp.sum(group_log, axis=1)
    after = jnp.concatenate([after, after], axis=1)[:, None, :]
    summary = summarise(frames, proj, log_decay, after)
    entering = enter_states(summary, total_log, shard_count)
    skip = per_channel(skip_gain)[None]
    return mix(slots, frames, proj, log_decay, skip, entering)


def solution(mesh):
    return jax.shard_map(
        functools.partial(shards, mesh.shape["seq"]),
        mesh=mesh,
        in_specs=(P("seq", "head"), P("head", "seq"), P("head", "seq"), P("head"), P("seq")),
        out_specs=P("seq", "head"),
        check_vma=False,
    )
```

time: 481 us -> 161 us (0.33)
  the two profiles are of different devices: /device:TPU:24 before, /device:TPU:0 now
where the time goes in v1:
time: 161 us
  Pallas kernels  64.6 us (40%)
  waiting for transfers between devices  33.4 us (21%)
  blocking collectives  22.2 us (14%)
  between operations  14.2 us (9%)
  local copies, waits for them, and re-layouts  9.6 us (6%)
  starting transfers between devices  9.01 us (6%)
  other arithmetic  7.8 us (5%)
    pallas_call x1, Pallas kernels, mix(): pl.pallas_call(mix_kernel, grid_spec=grid_spec, out_shape=jax.ShapeDtypeS...  37.1 us
    pallas_call x1, Pallas kernels, summarise(): pl.pallas_call(summary_kernel, grid=(groups,), in_specs=[pl.BlockSpec((GR...  27.5 us
    unnamed x1, blocking collectives  22.2 us
    all_gather x1, waiting for transfers between devices, shards(): proj = lax.all_gather(state_proj, 'head', axis=0, tiled=True)  21.7 us
    all_to_all x1, waiting for transfers between devices, enter_states(): lax.all_to_all(entering, 'seq', split_axis=0, concat_axis=1, tiled=True)  11 us
    unnamed x21, local copies, waits for them, and re-layouts  5.86 us
    all_to_all x1, starting transfers between devices, enter_states(): lax.all_to_all(summary[None], 'seq', split_axis=1, concat_axis=0, tiled=T...  5.52 us
    unnamed x1, other arithmetic  3.7 us
  transfers between devices with their start and end apart: 3, of which 2 were waited for; matrix products, arithmetic and copies ran while one was open for 3% of the time, Pallas kernels for 0%

profile of v1, /device:TPU:0, one launch (start us, length us, event | category | flops | bytes accessed | tf_op | source)
XLA Modules:
  0.0 160.9 jit_solution(4594601958851488970)
XLA Ops:
  6.5 0.7 all-gather.3.cloned.1.call-update
  7.3 1.1 reshape.58
  8.4 0.1 reduce_sum.47
  8.5 0.1 copy.8
  8.6 0.8 broadcast_compare_fusion
  9.4 0.1 select_reduce_fusion
  9.5 0.1 pad_maximum_fusion
  9.6 21.7 %all-gather.3.cloned.1.call-done.proj_ref = bf16[256,3072]{1,0:T(8,128)(2,1)} async-done(((bf16[64,3072]{1,0:T(8,128)(2,1)}), bf16[256,3072]{1,0:T(8,128)(2,1)}) %all-gather.3.cloned.1.call-update) | async-done | bytes 1572880 | tf_op jit(solution)/shard_map/all_gather | solution.py:206
  31.3 1.4 copy-done
  32.7 1.0 copy-done.2
  33.7 27.5 %summary.1 = bf16[128,2048]{1,0:T(8,128)(2,1)S(1)} custom-call(bf16[3072,2048]{1,0:T(8,128)(2,1)} %x_ref.3, bf16[256,3072]{1,0:T(8,128)(2,1)S(1)} %copy-done, f32[32,3072]{1,0:T(8,128)S(1)} %copy-done.2, f32[12,1,64]{2,1,0:T(1,128)S(1)} %broadcast_in_dim.88.after_ref), custom_call_target="tpu_custom_call" | custom-call | flops 3221225472 | bytes 12582912 | tf_op jit(solution)/shard_map/summary/pallas_call | solution.py:79
  61.3 0.8 copy.12
  62.1 0.5 broadcast.24
  62.6 3.7 %reduce.2 = bf16[128,2048]{1,0:T(8,128)(2,1)S(1)} reduce(bf16[128,1,2048]{2,1,0:T(2,128)(2,1)S(1)} %bitcast.12, bf16[]{:T(256)} %broadcast.24), dimensions={1}, to_apply=%bitcast.9.reduce_sub_computation | reduce | bytes 1048578
  66.3 1.2 reshape.67
  67.5 5.5 %all-to-all-start = ((bf16[8,2,16384]{2,1,0:T(2,128)(2,1)}), bf16[8,2,16384]{2,1,0:T(2,128)(2,1)S(1)}, u32[]{:S(2)}, u32[]{:S(2)}) async-start(bf16[8,2,16384]{2,1,0:T(2,128)(2,1)} %reshape.67), calls=%async_computation | async-start | bytes 1048576 | tf_op jit(solution)/shard_map/all_to_all | solution.py:191
  73.0 0.1 reduce_sum.46
  73.2 0.6 dynamic-slice
  74.4 0.2 dynamic-update-slice
  74.7 22.2 %all-reduce = f32[256]{0:T(256)S(1)} all-reduce(f32[256]{0:T(256)S(1)} %dynamic-update-slice), channel_id=2, replica_groups=mesh['seq'=8,'head'=4] {'seq'}, use_global_device_ids=true, to_apply=%add | all-reduce | flops 256 | bytes 2048
  96.9 0.1 reshape.61
  97.0 0.1 exponential_select_fusion
  97.1 0.3 broadcast_in_dim.84
  97.4 1.2 mul.19
  98.6 0.5 reshape.68
  99.2 0.4 copy.10
  99.5 2.6 %multiply_reduce_fusion = bf16[8,16,2048]{2,1,0:T(8,128)(2,1)} fusion(f32[8,16,2048]{2,1,0:T(8,128)S(1)} %bitcast.13, f32[8,8,2048]{2,1,0:T(8,128)} %mul.19), kind=kLoop, calls=%fused_computation | loop fusion | flops 3932160 | bytes 2097152 | tf_op jit(solution)/shard_map/reduce_sum | solution.py:199
  102.1 3.5 %all-to-all-start.1 = ((bf16[8,16,2048]{2,1,0:T(8,128)(2,1)}), bf16[8,16,2048]{2,1,0:T(8,128)(2,1)S(1)}, u32[]{:S(2)}, u32[]{:S(2)}) async-start(bf16[8,16,2048]{2,1,0:T(8,128)(2,1)} %multiply_reduce_fusion), calls=%async_computation.1 | async-start | bytes 1048576 | tf_op jit(solution)/shard_map/all_to_all | solution.py:201
  105.7 0.1 broadcast_in_dim_reshape.4.skip_ref
  105.8 0.1 select_reduce_fusion.1.slot_ref
  105.9 11.0 %all-to-all-done.1 = bf16[8,16,2048]{2,1,0:T(8,128)(2,1)S(1)} async-done(((bf16[8,16,2048]{2,1,0:T(8,128)(2,1)}), bf16[8,16,2048]{2,1,0:T(8,128)(2,1)S(1)}, u32[]{:S(2)}, u32[]{:S(2)}) %all-to-all-start.1) | async-done | bytes 524320 | tf_op jit(solution)/shard_map/all_to_all | solution.py:201
  116.9 37.1 %mix.1 = bf16[3072,2048]{1,0:T(8,128)(2,1)} custom-call(s32[12]{0:T(128)S(1)} %select_reduce_fusion.1.slot_ref, bf16[3072,2048]{1,0:T(8,128)(2,1)} %x_ref.3, bf16[256,3072]{1,0:T(8,128)(2,1)S(1)} %copy-done.1, f32[32,3072]{1,0:T(8,128)S(1)} %copy-done.3, f32[1,2048]{1,0:T(1,128)S(1)} %broadcast_in_dim_reshape.4.skip_ref, bf16[128,2048]{1,0:T(8,128)(2,1)S(1)} %bitcast.11), custom_call_target="tpu_custom_call" | custom-call | flops 6442450944 | bytes 25165824 | tf_op jit(solution)/shard_map/mix/pallas_call | solution.py:171
  (21 shorter events, 0.2 us)
Async XLA Ops:
  6.5 24.8 %all-gather.3.cloned.1.call-start = ((), (), s32[]{:S(2)}) async-start(), calls=%async_computation.2 | async-start | bytes 1966080 | tf_op jit(solution)/shard_map/all_gather | solution.py:206
  31.3 1.4 copy-start
  32.7 1.0 copy-start.2
  33.7 39.3 %copy-start.3 = (f32[32,3072]{1,0:T(8,128)S(1)}, f32[32,3072]{1,0:T(8,128)}, u32[]{:S(2)}) copy-start(f32[32,3072]{1,0:T(8,128)} %log_ref.3) | copy-start | bytes 1179652
  33.7 39.5 %copy-start.6 = (u32[32]{0:T(128)S(1)}, u32[32]{0:T(128)}, u32[]{:S(2)}) copy-start(u32[32]{0:T(128)} %constant.18) | copy-start | bytes 388
  61.3 44.4 %copy-start.5 = (f32[32]{0:T(128)S(1)}, f32[32]{0:T(128)}, u32[]{:S(2)}) copy-start(f32[32]{0:T(128)} %param.8) | copy-start | bytes 388
  61.3 44.5 %copy-start.4 = (s32[12]{0:T(128)S(1)}, s32[12]{0:T(128)}, u32[]{:S(2)}) copy-start(s32[12]{0:T(128)} %param.9) | copy-start | bytes 148
  61.3 55.6 %copy-start.1 = (bf16[256,3072]{1,0:T(8,128)(2,1)S(1)}, bf16[256,3072]{1,0:T(8,128)(2,1)}, u32[]{:S(2)}) copy-start(bf16[256,3072]{1,0:T(8,128)(2,1)} %all-gather.3.cloned.1.call-done.proj_ref) | copy-start | bytes 4718596
  67.5 31.1 %all-to-all-start = ((bf16[8,2,16384]{2,1,0:T(2,128)(2,1)}), bf16[8,2,16384]{2,1,0:T(2,128)(2,1)S(1)}, u32[]{:S(2)}, u32[]{:S(2)}) async-start(bf16[8,2,16384]{2,1,0:T(2,128)(2,1)} %reshape.67), calls=%async_computation | async-start | bytes 1048576 | tf_op jit(solution)/shard_map/all_to_all | solution.py:191
  102.1 14.8 %all-to-all-start.1 = ((bf16[8,16,2048]{2,1,0:T(8,128)(2,1)}), bf16[8,16,2048]{2,1,0:T(8,128)(2,1)S(1)}, u32[]{:S(2)}, u32[]{:S(2)}) async-start(bf16[8,16,2048]{2,1,0:T(8,128)(2,1)} %multiply_reduce_fusion), calls=%async_computation.1 | async-start | bytes 1048576 | tf_op jit(solution)/shard_map/all_to_all | solution.py:201
Sparse Core Ops, SparseCore 0:
  8.9 22.3 all-gather.2

commit v2 on v1

v2 whole, which is shorter than its diff:
```python
import functools

import jax
import jax.numpy as jnp
from jax import lax
from jax.experimental import pallas as pl
from jax.experimental.pallas import tpu as pltpu
from jax.sharding import PartitionSpec as P

HEAD_DIM = 64
STATE = 128
GROUP = 256
CHUNK = 128
TILE = 256
PIECES = 2
DECAY_ROWS = 2 * CHUNK + 16
MESH = pl.DeviceIdType.MESH
VMEM_BYTES = 48 * 1024 * 1024


def spread_matrix(heads, columns):
    rows = lax.broadcasted_iota(jnp.int32, (2 * heads, columns), 0) % heads
    owner = lax.broadcasted_iota(jnp.int32, (2 * heads, columns), 1) // HEAD_DIM
    return (rows == owner).astype(jnp.float32).astype(jnp.bfloat16)


def lower_matrix(length):
    rows = lax.broadcasted_iota(jnp.int32, (length, length), 0)
    columns = lax.broadcasted_iota(jnp.int32, (length, length), 1)
    return rows >= columns


def select_sums(mask, values, value_dim):
    high = values.astype(jnp.bfloat16)
    rest = values - high.astype(jnp.float32)
    middle = rest.astype(jnp.bfloat16)
    low = (rest - middle.astype(jnp.float32)).astype(jnp.bfloat16)
    total = None
    for term in (low, middle, high):
        part = lax.dot_general(
            mask, term, (((1,), (value_dim,)), ((), ())), preferred_element_type=jnp.float32
        )
        total = part if total is None else total + part
    return total


def two_terms(values, heads):
    high = values.astype(jnp.bfloat16).astype(jnp.float32)
    lanes = lax.broadcasted_iota(jnp.int32, values.shape, 1)
    return jnp.where(lanes < heads, high, values - high).astype(jnp.bfloat16)


def enter_kernel(
    shard_count,
    head_count,
    frames_ref,
    proj_ref,
    log_ref,
    onward_ref,
    enter_ref,
    input_ref,
    left_ref,
    decay_ref,
    x_ref,
    whole_ref,
    running_ref,
    group_log_ref,
    spread_ref,
    own_ref,
    own_send_ref,
    twin_ref,
    prior_ref,
    next_ref,
    total_ref,
    twin_total_ref,
    rates_ref,
    x_sems,
    proj_send,
    proj_recv,
    twin_send,
    twin_recv,
    next_send,
    next_recv,
    total_sems,
):
    shard = lax.axis_index("seq")
    head = lax.axis_index("head")
    shard_pair, shard_side = shard // 2, shard % 2
    head_pair, head_side = head // 2, head % 2
    shard_pairs, head_pairs = shard_count // 2, head_count // 2
    shard_twin = shard_pair * 2 + 1 - shard_side
    head_twin = head_pair * 2 + 1 - head_side
    has_prior = shard_pair > 0
    has_next = shard_pair < shard_pairs - 1
    shard_prior = jnp.where(has_prior, shard - 2, shard)
    shard_next = jnp.where(has_next, shard + 2, shard)
    frame_count, columns = x_ref.shape
    groups = frame_count // GROUP
    heads = log_ref.shape[0]
    slices = columns // TILE
    piece = frame_count // PIECES

    def read_frames(group):
        rows = pl.ds(pl.multiple_of(group * GROUP, GROUP), GROUP)
        return pltpu.make_async_copy(frames_ref.at[rows], x_ref.at[rows], x_sems.at[group])

    for group in range(groups):
        read_frames(group).start()

    barrier = pltpu.get_barrier_semaphore()

    def greet(device_id):
        pl.semaphore_signal(barrier, inc=1, device_id=device_id, device_id_type=MESH)

    for away in range(1, head_pairs):
        greet({"head": (head_pair + away) % head_pairs * 2 + head_side})
    greet({"head": head_twin})
    greet({"seq": shard_twin})

    @pl.when(has_prior)
    def _():
        greet({"seq": shard_prior})

    @pl.when(has_next)
    def _():
        greet({"seq": shard_next})

    neighbours = head_pairs + 1 + has_prior.astype(jnp.int32) + has_next.astype(jnp.int32)
    pl.semaphore_wait(barrier, neighbours)

    def send_proj(source, owner, target, place, part):
        columns_here = pl.ds(part * piece, piece)
        return pltpu.make_async_remote_copy(
            src_ref=source.at[:, columns_here],
            dst_ref=whole_ref.at[owner, :, columns_here],
            send_sem=proj_send.at[place, part],
            recv_sem=proj_recv.at[owner, part],
            device_id={"head": target},
            device_id_type=MESH,
        )

    proj_copies = []
    for part in range(PIECES):
        for away in range(1, head_pairs):
            target = (head_pair + away) % head_pairs * 2 + head_side
            proj_copies.append(send_proj(proj_ref, head, target, away, part))
            proj_copies[-1].start()
    for part in range(PIECES):
        proj_copies.append(send_proj(proj_ref, head, head_twin, 0, part))
        proj_copies[-1].start()
    whole_ref[head] = proj_ref[...]

    spread_ref[...] = spread_matrix(heads, columns)
    half = CHUNK // 2
    lower = lower_matrix(GROUP).astype(jnp.float32).astype(jnp.bfloat16)

    def sum_group(group, carry):
        frames_here = pl.ds(pl.multiple_of(group * GROUP, GROUP), GROUP)
        logs = log_ref[:, frames_here]
        running = select_sums(lower, jnp.concatenate([logs, logs], axis=0), 1)
        running_ref[frames_here] = running
        group_log_ref[group] = running[GROUP - 1 :]
        for chunk in range(GROUP // CHUNK):
            first = chunk * CHUNK
            here = running[first : first + CHUNK]
            before = running[first - 1 : first] if chunk else jnp.zeros_like(running[:1])
            middle = here[half - 1 : half]
            last = here[CHUNK - 1 :]
            extra = lax.broadcasted_iota(jnp.int32, (16, 2 * heads), 0)
            exponents = jnp.concatenate(
                [
                    middle - here,
                    here - middle,
                    jnp.where(extra == 0, middle - before, last - middle),
                ],
                axis=0,
            )
            decay_ref[group * (GROUP // CHUNK) + chunk] = two_terms(jnp.exp(exponents), heads)
        return carry

    lax.fori_loop(0, groups, sum_group, 0)
    group_logs = jnp.concatenate([group_log_ref[group] for group in range(groups)], axis=0)
    total = jnp.sum(group_logs, axis=0, keepdims=True)
    total_ref[...] = jnp.zeros_like(total_ref)
    total_ref[:, : 2 * heads] = jnp.broadcast_to(total, (8, 2 * heads))
    total_copy = pltpu.make_async_remote_copy(
        src_ref=total_ref,
        dst_ref=twin_total_ref,
        send_sem=total_sems.at[0],
        recv_sem=total_sems.at[1],
        device_id={"seq": shard_twin},
        device_id_type=MESH,
    )
    total_copy.start()
    after = select_sums(onward_ref[...].astype(jnp.bfloat16), group_logs, 0)
    for group in range(groups):
        group_log_ref[group] = after[group : group + 1]

    def scale_group(group, carry):
        read_frames(group).wait()
        rows = pl.ds(pl.multiple_of(group * GROUP, GROUP), GROUP)
        decay = two_terms(jnp.exp(group_log_ref[group] - running_ref[rows]), heads)
        for start in range(0, columns, TILE):
            tile = slice(start, start + TILE)
            wide = jnp.dot(decay, spread_ref[:, tile], preferred_element_type=jnp.float32)
            x_ref[rows, tile] = (x_ref[rows, tile].astype(jnp.float32) * wide).astype(jnp.bfloat16)
        return carry

    lax.fori_loop(0, groups, scale_group, 0)

    for part in range(PIECES):
        for away in range(1, head_pairs):
            owner = (head_pair + away) % head_pairs * 2 + head_side
            send_proj(proj_ref, owner, head_twin, 0, part).wait_recv()
            forward = send_proj(whole_ref.at[owner], owner, head_twin, head_pairs + away - 1, part)
            proj_copies.append(forward)
            forward.start()
    for part in range(PIECES):
        for pair in range(head_pairs):
            owner = pair * 2 + 1 - head_side
            send_proj(proj_ref, owner, head_twin, 0, part).wait_recv()
    rows_each = proj_ref.shape[0]
    for owner in range(head_pairs):
        input_ref[owner * rows_each : (owner + 1) * rows_each] = whole_ref[owner]

    total_copy.wait()
    both_totals = jnp.concatenate([total_ref[:, : 2 * heads], twin_total_ref[:, : 2 * heads]], axis=0)
    rates_ref[...] = jnp.dot(
        two_terms(jnp.exp(both_totals), heads), spread_ref[...], preferred_element_type=jnp.float32
    )

    def twin_copy(index):
        return pltpu.make_async_remote_copy(
            src_ref=own_send_ref.at[index],
            dst_ref=twin_ref.at[index],
            send_sem=twin_send.at[index],
            recv_sem=twin_recv.at[index],
            device_id={"seq": shard_twin},
            device_id_type=MESH,
        )

    def next_copy(index):
        return pltpu.make_async_remote_copy(
            src_ref=next_ref.at[index],
            dst_ref=prior_ref.at[index],
            send_sem=next_send.at[index],
            recv_sem=next_recv.at[index],
            device_id={"seq": shard_next},
            device_id_type=MESH,
        )

    def summarise(index, carry):
        tile = pl.ds(pl.multiple_of(index * TILE, TILE), TILE)
        own = jnp.dot(input_ref[...], x_ref[:, tile], preferred_element_type=jnp.float32)
        own_ref[index] = own
        own_send_ref[index] = own.astype(jnp.bfloat16)
        twin_copy(index).start()
        return carry

    lax.fori_loop(0, slices, summarise, 0)

    @pl.when(jnp.logical_not(has_prior))
    def _():
        prior_ref[...] = jnp.zeros_like(prior_ref)

    causal = lower_matrix(CHUNK)
    chunks = frame_count // CHUNK

    def couple(chunk, carry):
        frames_here = pl.ds(pl.multiple_of(chunk * CHUNK, CHUNK), CHUNK)
        output_rows = whole_ref[head_pairs:, :, frames_here].reshape(STATE, CHUNK)
        output_map = output_rows.astype(jnp.float32).T.astype(jnp.bfloat16)
        coupling = jnp.dot(
            output_map, input_ref[:, frames_here], preferred_element_type=jnp.float32
        )
        left_ref[chunk, :, :CHUNK] = jnp.where(causal, coupling, 0.0).astype(jnp.bfloat16)
        left_ref[chunk, :, CHUNK:] = output_map
        return carry

    first_side = shard_side == 0

    def hand_on(index, carry):
        tile = pl.ds(pl.multiple_of(index * TILE, TILE), TILE)
        own_rate = rates_ref[0:1, tile]
        twin_rate = rates_ref[8:9, tile]
        twin_copy(index).wait_recv()

        @pl.when(has_prior)
        def _():
            next_copy(index).wait_recv()

        own = own_ref[index]
        twin = twin_ref[index].astype(jnp.float32)
        prior = prior_ref[index].astype(jnp.float32)

        @pl.when(has_next)
        def _():
            pair_sum = jnp.where(first_side, twin_rate * own + twin, own_rate * twin + own)
            next_ref[index] = (own_rate * twin_rate * prior + pair_sum).astype(jnp.bfloat16)
            next_copy(index).start()

        enter_ref[:, tile] = jnp.where(first_side, prior, twin_rate * prior + twin).astype(
            jnp.bfloat16
        )
        lax.fori_loop(chunks * index // slices, chunks * (index + 1) // slices, couple, 0)
        return carry

    lax.fori_loop(0, slices, hand_on, 0)

    def finish(index, carry):
        twin_copy(index).wait_send()

        @pl.when(has_next)
        def _():
            next_copy(index).wait_send()

        return carry

    lax.fori_loop(0, slices, finish, 0)
    for copy in proj_copies:
        copy.wait_send()


def enter_states(shard_count, head_count, frames, state_proj, logs, onward):
    frame_count, columns = frames.shape
    heads = logs.shape[0]
    groups = frame_count // GROUP
    chunks = frame_count // CHUNK
    slices = columns // TILE
    vmem = pl.BlockSpec(memory_space=pltpu.VMEM)
    dma = pltpu.SemaphoreType.DMA
    return pl.pallas_call(
        functools.partial(enter_kernel, shard_count, head_count),
        in_specs=[pl.BlockSpec(memory_space=pl.ANY), vmem, vmem, vmem],
        out_specs=[vmem] * 4,
        out_shape=[
            jax.ShapeDtypeStruct((STATE, columns), jnp.bfloat16),
            jax.ShapeDtypeStruct((STATE, frame_count), jnp.bfloat16),
            jax.ShapeDtypeStruct((chunks, CHUNK, 2 * CHUNK), jnp.bfloat16),
            jax.ShapeDtypeStruct((chunks, DECAY_ROWS, 2 * heads), jnp.bfloat16),
        ],
        scratch_shapes=[
            pltpu.VMEM((frame_count, columns), jnp.bfloat16),
            pltpu.VMEM((head_count,) + state_proj.shape, jnp.bfloat16),
            pltpu.VMEM((frame_count, 2 * heads), jnp.float32),
            pltpu.VMEM((groups, 1, 2 * heads), jnp.float32),
            pltpu.VMEM((2 * heads, columns), jnp.bfloat16),
            pltpu.VMEM((slices, STATE, TILE), jnp.float32),
            pltpu.VMEM((slices, STATE, TILE), jnp.bfloat16),
            pltpu.VMEM((slices, STATE, TILE), jnp.bfloat16),
            pltpu.VMEM((slices, STATE, TILE), jnp.bfloat16),
            pltpu.VMEM((slices, STATE, TILE), jnp.bfloat16),
            pltpu.VMEM((8, 128), jnp.float32),
            pltpu.VMEM((8, 128), jnp.float32),
            pltpu.VMEM((16, columns), jnp.float32),
            dma((groups,)),
            dma((head_count, PIECES)),
            dma((head_count, PIECES)),
            dma((slices,)),
            dma((slices,)),
            dma((slices,)),
            dma((slices,)),
            dma((2,)),
        ],
        compiler_params=pltpu.CompilerParams(
            collective_id=0, has_side_effects=True, vmem_limit_bytes=VMEM_BYTES
        ),
        cost_estimate=pl.CostEstimate(
            flops=4 * frame_count * columns * STATE,
            bytes_accessed=2 * frame_count * columns,
            transcendentals=frame_count * heads,
        ),
        name="enter",
    )(frames, state_proj, logs, onward)


def mix_kernel(
    slot_ref, x_ref, left_ref, input_ref, decay_ref, skip_ref, enter_ref, out_ref, state_ref, spread_ref, both_ref
):
    step = pl.program_id(0)
    columns = x_ref.shape[1]
    heads = columns // HEAD_DIM

    @pl.when(step == 0)
    def _():
        state_ref[...] = enter_ref[...].astype(jnp.float32)
        spread_ref[...] = spread_matrix(heads, columns)

    for chunk in range(GROUP // CHUNK):
        rows = slice(chunk * CHUNK, (chunk + 1) * CHUNK)
        for start in range(0, columns, TILE):
            tile = slice(start, start + TILE)
            wide = jnp.dot(decay_ref[chunk], spread_ref[:, tile], preferred_element_type=jnp.float32)
            x = x_ref[rows, tile].astype(jnp.float32)
            scaled = (x * wide[:CHUNK]).astype(jnp.bfloat16)
            prior = state_ref[:, tile] * wide[2 * CHUNK : 2 * CHUNK + 1]
            both_ref[chunk, :CHUNK, tile] = scaled
            both_ref[chunk, CHUNK:, tile] = prior.astype(jnp.bfloat16)
            mixed = jnp.dot(left_ref[chunk], both_ref[chunk, :, tile], preferred_element_type=jnp.float32)
            out_ref[rows, tile] = (
                mixed * wide[CHUNK : 2 * CHUNK] + skip_ref[:, tile] * x
            ).astype(out_ref.dtype)
            update = jnp.dot(input_ref[:, rows], scaled, preferred_element_type=jnp.float32)
            state_ref[:, tile] = (prior + update) * wide[2 * CHUNK + 1 : 2 * CHUNK + 2]


def mix(slots, frames, left, input_map, decay, skip, entering):
    frame_count, columns = frames.shape
    heads = columns // HEAD_DIM
    groups = frame_count // GROUP
    each = GROUP // CHUNK
    grid_spec = pltpu.PrefetchScalarGridSpec(
        num_scalar_prefetch=1,
        grid=(groups,),
        in_specs=[
            pl.BlockSpec((GROUP, columns), lambda i, slot: (slot[i], 0)),
            pl.BlockSpec((each,) + left.shape[1:], lambda i, slot: (slot[i], 0, 0)),
            pl.BlockSpec((STATE, GROUP), lambda i, slot: (0, slot[i])),
            pl.BlockSpec((each,) + decay.shape[1:], lambda i, slot: (slot[i], 0, 0)),
            pl.BlockSpec((1, columns), lambda i, slot: (0, 0)),
            pl.BlockSpec((STATE, columns), lambda i, slot: (0, 0)),
        ],
        out_specs=pl.BlockSpec((GROUP, columns), lambda i, slot: (i, 0)),
        scratch_shapes=[
            pltpu.VMEM((STATE, columns), jnp.float32),
            pltpu.VMEM((2 * heads, columns), jnp.bfloat16),
            pltpu.VMEM((each, CHUNK + STATE, columns), jnp.bfloat16),
        ],
    )
    return pl.pallas_call(
        mix_kernel,
        grid_spec=grid_spec,
        out_shape=jax.ShapeDtypeStruct((frame_count, columns), jnp.bfloat16),
        compiler_params=pltpu.CompilerParams(vmem_limit_bytes=VMEM_BYTES),
        cost_estimate=pl.CostEstimate(
            flops=8 * frame_count * columns * STATE,
            bytes_accessed=4 * frame_count * columns,
            transcendentals=2 * frame_count * heads,
        ),
        name="mix",
    )(slots, frames, left, input_map, decay, skip, entering)


def shards(shard_count, head_count, frames, state_proj, log_decay, skip_gain, group_pos):
    groups = group_pos.shape[0]
    place = group_pos - lax.axis_index("seq") * groups
    slot_ids = jnp.arange(groups, dtype=jnp.int32)
    slots = jnp.sum(jnp.where(place[:, None] == slot_ids[None, :], slot_ids[:, None], 0), axis=0)
    onward = (group_pos[None, :] >= group_pos[:, None]).astype(jnp.float32)
    entering, input_map, left, decay = enter_states(
        shard_count, head_count, frames, state_proj, log_decay, onward
    )
    skip = jnp.repeat(skip_gain, HEAD_DIM)[None]
    return mix(slots, frames, left, input_map, decay, skip, entering)


def solution(mesh):
    return jax.shard_map(
        functools.partial(shards, mesh.shape["seq"], mesh.shape["head"]),
        mesh=mesh,
        in_specs=(P("seq", "head"), P("head", "seq"), P("head", "seq"), P("head"), P("seq")),
        out_specs=P("seq", "head"),
        check_vma=False,
    )
```

time: 161 us -> 84.4 us (0.52)
  the two profiles are of different devices: /device:TPU:0 before, /device:TPU:24 now
where the time goes in v2:
time: 84.4 us; the launch traced here: 84.2 us
  Pallas kernels  79.8 us (95%)
  local copies, waits for them, and re-layouts  2.8 us (3%)
  other arithmetic  1.55 us (2%)
    pallas_call x1, Pallas kernels, mix(): pl.pallas_call(mix_kernel, grid_spec=grid_spec, out_shape=jax.ShapeDtypeS...  43.2 us
    pallas_call x1, Pallas kernels, enter_states(): pl.pallas_call(functools.partial(enter_kernel, shard_count, head_count),...  36.6 us
    unnamed x4, local copies, waits for them, and re-layouts  1.99 us

profile of v2, /device:TPU:24, one launch (start us, length us, event | category | flops | bytes accessed | tf_op | source)
XLA Modules:
  0.0 84.2 jit_solution(16943531661269186235)
XLA Ops:
  0.0 0.7 broadcast_subtract_fusion
  0.7 0.1 select_reduce_fusion.slot_ref
  0.7 0.8 compare_convert_fusion.onward_ref
  1.5 0.7 broadcast_in_dim.22
  2.3 0.1 broadcast_in_dim_reshape.3.skip_ref
  2.4 0.0 copy-start
  2.4 1.0 %copy-done = bf16[64,3072]{1,0:T(8,128)(2,1)S(1)} copy-done((bf16[64,3072]{1,0:T(8,128)(2,1)S(1)}, bf16[64,3072]{1,0:T(8,128)(2,1)}, u32[]{:S(2)}) %copy-start) | copy-done | bytes 393240
  3.4 0.0 copy-start.1
  3.4 1.0 %copy-done.1 = f32[32,3072]{1,0:T(8,128)S(1)} copy-done((f32[32,3072]{1,0:T(8,128)S(1)}, f32[32,3072]{1,0:T(8,128)}, u32[]{:S(2)}) %copy-start.1) | copy-done | bytes 393240
  4.4 36.6 %enter.1 = (bf16[128,2048]{1,0:T(8,128)(2,1)S(1)}, bf16[128,3072]{1,0:T(8,128)(2,1)S(1)}, bf16[24,128,256]{2,1,0:T(8,128)(2,1)S(1)}, bf16[24,272,64]{2,1,0:T(8,128)(2,1)S(1)}) custom-call(bf16[3072,2048]{1,0:T(8,128)(2,1)} %x_ref.1, bf16[64,3072]{1,0:T(8,128)(2,1)S(1)} %copy-done, f32[32,3072]{1,0:T(8,128)S(1)} %copy-done.1, ...), custom_call_target="tpu_custom_call" | custom-call | flops 3221225472 | bytes 12582912 | tf_op jit(solution)/shard_map/enter/pallas_call | solution.py:332
  41.0 43.2 %mix.1 = bf16[3072,2048]{1,0:T(8,128)(2,1)} custom-call(s32[12]{0:T(128)S(1)} %select_reduce_fusion.slot_ref, bf16[3072,2048]{1,0:T(8,128)(2,1)} %x_ref.1, bf16[24,128,256]{2,1,0:T(8,128)(2,1)S(1)} %get-tuple-element.9.left_ref, bf16[128,3072]{1,0:T(8,128)(2,1)S(1)} %get-tuple-element.10.input_ref, bf16[24,272,64]{2,1,0:T(8,128)(2,1)S(1)} %get-tuple-element.11.decay_ref, ...), custom_call_target="tpu_custom_call" | custom-call | flops 6442450944 | bytes 25165824 | tf_op jit(solution)/shard_map/mix/pallas_call | solution.py:430
Async XLA Ops:
  2.4 1.0 %copy-start = (bf16[64,3072]{1,0:T(8,128)(2,1)S(1)}, bf16[64,3072]{1,0:T(8,128)(2,1)}, u32[]{:S(2)}) copy-start(bf16[64,3072]{1,0:T(8,128)(2,1)} %proj_ref.1) | copy-start | bytes 1179652
  3.4 1.0 %copy-start.1 = (f32[32,3072]{1,0:T(8,128)S(1)}, f32[32,3072]{1,0:T(8,128)}, u32[]{:S(2)}) copy-start(f32[32,3072]{1,0:T(8,128)} %log_ref.1) | copy-start | bytes 1179652

commit v3 on v2

--- a/solution.py
+++ b/solution.py
@@ -13,15 +13,26 @@
 CHUNK = 128
 TILE = 256
 PIECES = 2
-DECAY_ROWS = 2 * CHUNK + 16
+LANES = 128
+DECAY_ROWS = 2 * CHUNK + 8
 MESH = pl.DeviceIdType.MESH
 VMEM_BYTES = 48 * 1024 * 1024
 
 
 def spread_matrix(heads, columns):
-    rows = lax.broadcasted_iota(jnp.int32, (2 * heads, columns), 0) % heads
-    owner = lax.broadcasted_iota(jnp.int32, (2 * heads, columns), 1) // HEAD_DIM
-    return (rows == owner).astype(jnp.float32).astype(jnp.bfloat16)
+    rows = lax.broadcasted_iota(jnp.int32, (LANES, columns), 0)
+    owner = lax.broadcasted_iota(jnp.int32, (LANES, columns), 1) // HEAD_DIM
+    same = (rows % heads == owner) & (rows < 2 * heads)
+    return same.astype(jnp.float32).astype(jnp.bfloat16)
+
+
+def widen(values, start):
+    first = lax.broadcasted_iota(jnp.int32, values.shape, 1) // HEAD_DIM
+    parts = [
+        jnp.take_along_axis(values, first + at // HEAD_DIM, axis=1, mode="promise_in_bounds")
+        for at in range(start, start + TILE, LANES)
+    ]
+    return jnp.concatenate(parts, axis=1)
 
 
 def lower_matrix(length):
@@ -58,9 +69,9 @@
     log_ref,
     onward_ref,
     enter_ref,
-    input_ref,
     left_ref,
     decay_ref,
+    input_ref,
     x_ref,
     whole_ref,
     running_ref,
@@ -157,7 +168,7 @@
     def sum_group(group, carry):
         frames_here = pl.ds(pl.multiple_of(group * GROUP, GROUP), GROUP)
         logs = log_ref[:, frames_here]
-        running = select_sums(lower, jnp.concatenate([logs, logs], axis=0), 1)
+        running = select_sums(lower, jnp.concatenate([logs] * (LANES // heads), axis=0), 1)
         running_ref[frames_here] = running
         group_log_ref[group] = running[GROUP - 1 :]
         for chunk in range(GROUP // CHUNK):
@@ -166,7 +177,7 @@
             before = running[first - 1 : first] if chunk else jnp.zeros_like(running[:1])
             middle = here[half - 1 : half]
             last = here[CHUNK - 1 :]
-            extra = lax.broadcasted_iota(jnp.int32, (16, 2 * heads), 0)
+            extra = lax.broadcasted_iota(jnp.int32, (8, LANES), 0)
             exponents = jnp.concatenate(
                 [
                     middle - here,
@@ -175,14 +186,13 @@
                 ],
                 axis=0,
             )
-            decay_ref[group * (GROUP // CHUNK) + chunk] = two_terms(jnp.exp(exponents), heads)
+            decay_ref[group * (GROUP // CHUNK) + chunk] = jnp.exp(exponents)
         return carry
 
     lax.fori_loop(0, groups, sum_group, 0)
     group_logs = jnp.concatenate([group_log_ref[group] for group in range(groups)], axis=0)
     total = jnp.sum(group_logs, axis=0, keepdims=True)
-    total_ref[...] = jnp.zeros_like(total_ref)
-    total_ref[:, : 2 * heads] = jnp.broadcast_to(total, (8, 2 * heads))
+    total_ref[...] = jnp.broadcast_to(total, total_ref.shape)
     total_copy = pltpu.make_async_remote_copy(
         src_ref=total_ref,
         dst_ref=twin_total_ref,
@@ -224,7 +234,7 @@
         input_ref[owner * rows_each : (owner + 1) * rows_each] = whole_ref[owner]
 
     total_copy.wait()
-    both_totals = jnp.concatenate([total_ref[:, : 2 * heads], twin_total_ref[:, : 2 * heads]], axis=0)
+    both_totals = jnp.concatenate([total_ref[...], twin_total_ref[...]], axis=0)
     rates_ref[...] = jnp.dot(
         two_terms(jnp.exp(both_totals), heads), spread_ref[...], preferred_element_type=jnp.float32
     )
@@ -270,11 +280,12 @@
         frames_here = pl.ds(pl.multiple_of(chunk * CHUNK, CHUNK), CHUNK)
         output_rows = whole_ref[head_pairs:, :, frames_here].reshape(STATE, CHUNK)
         output_map = output_rows.astype(jnp.float32).T.astype(jnp.bfloat16)
-        coupling = jnp.dot(
-            output_map, input_ref[:, frames_here], preferred_element_type=jnp.float32
-        )
-        left_ref[chunk, :, :CHUNK] = jnp.where(causal, coupling, 0.0).astype(jnp.bfloat16)
-        left_ref[chunk, :, CHUNK:] = output_map
+        input_map = input_ref[:, frames_here]
+        coupling = jnp.dot(output_map, input_map, preferred_element_type=jnp.float32)
+        left_ref[chunk, :CHUNK, :CHUNK] = jnp.where(causal, coupling, 0.0).astype(jnp.bfloat16)
+        left_ref[chunk, :CHUNK, CHUNK:] = output_map
+        left_ref[chunk, CHUNK:, :CHUNK] = input_map
+        left_ref[chunk, CHUNK:, CHUNK:] = jnp.zeros((STATE, STATE), jnp.bfloat16)
         return carry
 
     first_side = shard_side == 0
@@ -332,19 +343,19 @@
     return pl.pallas_call(
         functools.partial(enter_kernel, shard_count, head_count),
         in_specs=[pl.BlockSpec(memory_space=pl.ANY), vmem, vmem, vmem],
-        out_specs=[vmem] * 4,
+        out_specs=[vmem] * 3,
         out_shape=[
             jax.ShapeDtypeStruct((STATE, columns), jnp.bfloat16),
-            jax.ShapeDtypeStruct((STATE, frame_count), jnp.bfloat16),
-            jax.ShapeDtypeStruct((chunks, CHUNK, 2 * CHUNK), jnp.bfloat16),
-            jax.ShapeDtypeStruct((chunks, DECAY_ROWS, 2 * heads), jnp.bfloat16),
+            jax.ShapeDtypeStruct((chunks, CHUNK + STATE, CHUNK + STATE), jnp.bfloat16),
+            jax.ShapeDtypeStruct((chunks, DECAY_ROWS, LANES), jnp.float32),
         ],
         scratch_shapes=[
+            pltpu.VMEM((STATE, frame_count), jnp.bfloat16),
             pltpu.VMEM((frame_count, columns), jnp.bfloat16),
             pltpu.VMEM((head_count,) + state_proj.shape, jnp.bfloat16),
-            pltpu.VMEM((frame_count, 2 * heads), jnp.float32),
-            pltpu.VMEM((groups, 1, 2 * heads), jnp.float32),
-            pltpu.VMEM((2 * heads, columns), jnp.bfloat16),
+            pltpu.VMEM((frame_count, LANES), jnp.float32),
+            pltpu.VMEM((groups, 1, LANES), jnp.float32),
+            pltpu.VMEM((LANES, columns), jnp.bfloat16),
             pltpu.VMEM((slices, STATE, TILE), jnp.float32),
             pltpu.VMEM((slices, STATE, TILE), jnp.bfloat16),
             pltpu.VMEM((slices, STATE, TILE), jnp.bfloat16),
@@ -374,37 +385,30 @@
     )(frames, state_proj, logs, onward)
 
 
-def mix_kernel(
-    slot_ref, x_ref, left_ref, input_ref, decay_ref, skip_ref, enter_ref, out_ref, state_ref, spread_ref, both_ref
-):
+def mix_kernel(slot_ref, x_ref, left_ref, decay_ref, skip_ref, enter_ref, out_ref, state_ref):
     step = pl.program_id(0)
     columns = x_ref.shape[1]
-    heads = columns // HEAD_DIM
 
     @pl.when(step == 0)
     def _():
         state_ref[...] = enter_ref[...].astype(jnp.float32)
-        spread_ref[...] = spread_matrix(heads, columns)
 
     for chunk in range(GROUP // CHUNK):
         rows = slice(chunk * CHUNK, (chunk + 1) * CHUNK)
         for start in range(0, columns, TILE):
             tile = slice(start, start + TILE)
-            wide = jnp.dot(decay_ref[chunk], spread_ref[:, tile], preferred_element_type=jnp.float32)
             x = x_ref[rows, tile].astype(jnp.float32)
-            scaled = (x * wide[:CHUNK]).astype(jnp.bfloat16)
-            prior = state_ref[:, tile] * wide[2 * CHUNK : 2 * CHUNK + 1]
-            both_ref[chunk, :CHUNK, tile] = scaled
-            both_ref[chunk, CHUNK:, tile] = prior.astype(jnp.bfloat16)
-            mixed = jnp.dot(left_ref[chunk], both_ref[chunk, :, tile], preferred_element_type=jnp.float32)
-            out_ref[rows, tile] = (
-                mixed * wide[CHUNK : 2 * CHUNK] + skip_ref[:, tile] * x
-            ).astype(out_ref.dtype)
-            update = jnp.dot(input_ref[:, rows], scaled, preferred_element_type=jnp.float32)
-            state_ref[:, tile] = (prior + update) * wide[2 * CHUNK + 1 : 2 * CHUNK + 2]
-
-
-def mix(slots, frames, left, input_map, decay, skip, entering):
+            scaled = x * widen(decay_ref[chunk, :CHUNK], start)
+            ends = widen(decay_ref[chunk, 2 * CHUNK :], start)
+            prior = state_ref[:, tile] * ends[0:1]
+            both = jnp.concatenate([scaled.astype(jnp.bfloat16), prior.astype(jnp.bfloat16)], axis=0)
+            sums = jnp.dot(left_ref[chunk], both, preferred_element_type=jnp.float32)
+            mixed = sums[:CHUNK] * widen(decay_ref[chunk, CHUNK : 2 * CHUNK], start)
+            out_ref[rows, tile] = (mixed + skip_ref[:, tile] * x).astype(out_ref.dtype)
+            state_ref[:, tile] = (prior + sums[CHUNK:]) * ends[1:2]
+
+
+def mix(slots, frames, left, decay, skip, entering):
     frame_count, columns = frames.shape
     heads = columns // HEAD_DIM
     groups = frame_count // GROUP
@@ -415,7 +419,6 @@
         in_specs=[
             pl.BlockSpec((GROUP, columns), lambda i, slot: (slot[i], 0)),
             pl.BlockSpec((each,) + left.shape[1:], lambda i, slot: (slot[i], 0, 0)),
-            pl.BlockSpec((STATE, GROUP), lambda i, slot: (0, slot[i])),
             pl.BlockSpec((each,) + decay.shape[1:], lambda i, slot: (slot[i], 0, 0)),
             pl.BlockSpec((1, columns), lambda i, slot: (0, 0)),
             pl.BlockSpec((STATE, columns), lambda i, slot: (0, 0)),
@@ -423,8 +426,6 @@
         out_specs=pl.BlockSpec((GROUP, columns), lambda i, slot: (i, 0)),
         scratch_shapes=[
             pltpu.VMEM((STATE, columns), jnp.float32),
-            pltpu.VMEM((2 * heads, columns), jnp.bfloat16),
-            pltpu.VMEM((each, CHUNK + STATE, columns), jnp.bfloat16),
         ],
     )
     return pl.pallas_call(
@@ -438,7 +439,7 @@
             transcendentals=2 * frame_count * heads,
         ),
         name="mix",
-    )(slots, frames, left, input_map, decay, skip, entering)
+    )(slots, frames, left, decay, skip, entering)
 
 
 def shards(shard_count, head_count, frames, state_proj, log_decay, skip_gain, group_pos):
@@ -447,11 +448,11 @@
     slot_ids = jnp.arange(groups, dtype=jnp.int32)
     slots = jnp.sum(jnp.where(place[:, None] == slot_ids[None, :], slot_ids[:, None], 0), axis=0)
     onward = (group_pos[None, :] >= group_pos[:, None]).astype(jnp.float32)
-    entering, input_map, left, decay = enter_states(
+    entering, left, decay = enter_states(
         shard_count, head_count, frames, state_proj, log_decay, onward
     )
     skip = jnp.repeat(skip_gain, HEAD_DIM)[None]
-    return mix(slots, frames, left, input_map, decay, skip, entering)
+    return mix(slots, frames, left, decay, skip, entering)
 
 
 def solution(mesh):

time: 84.4 us -> 67.6 us (0.80)
  Pallas kernels: 79.8 us -> 62.9 us
    pallas_call x1, Pallas kernels: 43.2 us -> 24.6 us  [mix(): pl.pallas_call(mix_kernel, grid_spec=grid_spec, out_shape=jax.ShapeDtypeS...]
    pallas_call x1, Pallas kernels: 36.6 us -> 38.3 us  [enter_states(): pl.pallas_call(functools.partial(enter_kernel, shard_count, head_count),...]
where the time goes in v3:
time: 67.6 us; the launch traced here: 67.3 us
  Pallas kernels  62.9 us (93%)
  local copies, waits for them, and re-layouts  2.8 us (4%)
  other arithmetic  1.55 us (2%)
    pallas_call x1, Pallas kernels, enter_states(): pl.pallas_call(functools.partial(enter_kernel, shard_count, head_count),...  38.3 us
    pallas_call x1, Pallas kernels, mix(): pl.pallas_call(mix_kernel, grid_spec=grid_spec, out_shape=jax.ShapeDtypeS...  24.6 us
    unnamed x4, local copies, waits for them, and re-layouts  1.99 us

profile of v3, /device:TPU:24, one launch (start us, length us, event | category | flops | bytes accessed | tf_op | source)
XLA Modules:
  0.0 67.3 jit_solution(14146089819907064477)
XLA Ops:
  0.0 0.7 broadcast_subtract_fusion
  0.7 0.1 select_reduce_fusion.slot_ref
  0.7 0.8 %compare_convert_fusion.onward_ref = f32[12,12]{1,0:T(8,128)S(1)} fusion(s32[12]{0:T(128)} %param.9), kind=kLoop, calls=%fused_computation.2 | loop fusion | flops 288 | bytes 624 | tf_op jit(solution)/shard_map/convert_element_type | solution.py:450
  1.5 0.7 %broadcast_in_dim.22 = f32[32,64]{1,0:T(8,128)S(1)} broadcast(f32[32]{0:T(128)} %param.8), dimensions={0} | broadcast | bytes 8320 | tf_op jit(solution)/shard_map/broadcast_in_dim | solution.py:454
  2.3 0.1 broadcast_in_dim_reshape.3.skip_ref
  2.4 0.0 copy-start
  2.4 1.0 %copy-done = bf16[64,3072]{1,0:T(8,128)(2,1)S(1)} copy-done((bf16[64,3072]{1,0:T(8,128)(2,1)S(1)}, bf16[64,3072]{1,0:T(8,128)(2,1)}, u32[]{:S(2)}) %copy-start) | copy-done | bytes 393240
  3.4 0.0 copy-start.1
  3.4 1.0 %copy-done.1 = f32[32,3072]{1,0:T(8,128)S(1)} copy-done((f32[32,3072]{1,0:T(8,128)S(1)}, f32[32,3072]{1,0:T(8,128)}, u32[]{:S(2)}) %copy-start.1) | copy-done | bytes 393240
  4.4 38.3 %enter.1 = (bf16[128,2048]{1,0:T(8,128)(2,1)S(1)}, bf16[24,256,256]{2,1,0:T(8,128)(2,1)S(1)}, f32[24,264,128]{2,1,0:T(8,128)}) custom-call(bf16[3072,2048]{1,0:T(8,128)(2,1)} %x_ref.1, bf16[64,3072]{1,0:T(8,128)(2,1)S(1)} %copy-done, f32[32,3072]{1,0:T(8,128)S(1)} %copy-done.1, f32[12,12]{1,0:T(8,128)S(1)} %compare_convert_fusion.onward_ref), custom_call_target="tpu_custom_call" | custom-call | flops 3221225472 | bytes 12582912 | tf_op jit(solution)/shard_map/enter/pallas_call | solution.py:343
  42.7 24.6 %mix.1 = bf16[3072,2048]{1,0:T(8,128)(2,1)} custom-call(s32[12]{0:T(128)S(1)} %select_reduce_fusion.slot_ref, bf16[3072,2048]{1,0:T(8,128)(2,1)} %x_ref.1, bf16[24,256,256]{2,1,0:T(8,128)(2,1)S(1)} %get-tuple-element.8.left_ref, f32[24,264,128]{2,1,0:T(8,128)} %get-tuple-element.9.decay_ref, f32[1,2048]{1,0:T(1,128)S(1)} %broadcast_in_dim_reshape.3.skip_ref, ...), custom_call_target="tpu_custom_call" | custom-call | flops 6442450944 | bytes 25165824 | tf_op jit(solution)/shard_map/mix/pallas_call | solution.py:431
Async XLA Ops:
  2.4 1.0 %copy-start = (bf16[64,3072]{1,0:T(8,128)(2,1)S(1)}, bf16[64,3072]{1,0:T(8,128)(2,1)}, u32[]{:S(2)}) copy-start(bf16[64,3072]{1,0:T(8,128)(2,1)} %proj_ref.1) | copy-start | bytes 1179652
  3.4 1.0 %copy-start.1 = (f32[32,3072]{1,0:T(8,128)S(1)}, f32[32,3072]{1,0:T(8,128)}, u32[]{:S(2)}) copy-start(f32[32,3072]{1,0:T(8,128)} %log_ref.1) | copy-start | bytes 1179652

commit v4 on v3

--- a/solution.py
+++ b/solution.py
@@ -75,7 +75,7 @@
     x_ref,
     whole_ref,
     running_ref,
-    group_log_ref,
+    leave_ref,
     spread_ref,
     own_ref,
     own_send_ref,
@@ -162,35 +162,13 @@
     whole_ref[head] = proj_ref[...]
 
     spread_ref[...] = spread_matrix(heads, columns)
-    half = CHUNK // 2
     lower = lower_matrix(GROUP).astype(jnp.float32).astype(jnp.bfloat16)
 
-    def sum_group(group, carry):
-        frames_here = pl.ds(pl.multiple_of(group * GROUP, GROUP), GROUP)
-        logs = log_ref[:, frames_here]
-        running = select_sums(lower, jnp.concatenate([logs] * (LANES // heads), axis=0), 1)
-        running_ref[frames_here] = running
-        group_log_ref[group] = running[GROUP - 1 :]
-        for chunk in range(GROUP // CHUNK):
-            first = chunk * CHUNK
-            here = running[first : first + CHUNK]
-            before = running[first - 1 : first] if chunk else jnp.zeros_like(running[:1])
-            middle = here[half - 1 : half]
-            last = here[CHUNK - 1 :]
-            extra = lax.broadcasted_iota(jnp.int32, (8, LANES), 0)
-            exponents = jnp.concatenate(
-                [
-                    middle - here,
-                    here - middle,
-                    jnp.where(extra == 0, middle - before, last - middle),
-                ],
-                axis=0,
-            )
-            decay_ref[group * (GROUP // CHUNK) + chunk] = jnp.exp(exponents)
-        return carry
-
-    lax.fori_loop(0, groups, sum_group, 0)
-    group_logs = jnp.concatenate([group_log_ref[group] for group in range(groups)], axis=0)
+    group_rows = [slice(group * GROUP, (group + 1) * GROUP) for group in range(groups)]
+    for rows in group_rows:
+        logs = log_ref[:, rows]
+        running_ref[rows] = select_sums(lower, jnp.concatenate([logs] * (LANES // heads), axis=0), 1)
+    group_logs = jnp.concatenate([running_ref[rows.stop - 1 : rows.stop] for rows in group_rows], axis=0)
     total = jnp.sum(group_logs, axis=0, keepdims=True)
     total_ref[...] = jnp.broadcast_to(total, total_ref.shape)
     total_copy = pltpu.make_async_remote_copy(
@@ -203,20 +181,9 @@
     )
     total_copy.start()
     after = select_sums(onward_ref[...].astype(jnp.bfloat16), group_logs, 0)
-    for group in range(groups):
-        group_log_ref[group] = after[group : group + 1]
-
-    def scale_group(group, carry):
-        read_frames(group).wait()
-        rows = pl.ds(pl.multiple_of(group * GROUP, GROUP), GROUP)
-        decay = two_terms(jnp.exp(group_log_ref[group] - running_ref[rows]), heads)
-        for start in range(0, columns, TILE):
-            tile = slice(start, start + TILE)
-            wide = jnp.dot(decay, spread_ref[:, tile], preferred_element_type=jnp.float32)
-            x_ref[rows, tile] = (x_ref[rows, tile].astype(jnp.float32) * wide).astype(jnp.bfloat16)
-        return carry
-
-    lax.fori_loop(0, groups, scale_group, 0)
+    for group, rows in enumerate(group_rows):
+        leaving = jnp.exp(after[group : group + 1] - running_ref[rows])
+        leave_ref[rows] = two_terms(leaving, heads)
 
     for part in range(PIECES):
         for away in range(1, head_pairs):
@@ -259,24 +226,30 @@
             device_id_type=MESH,
         )
 
-    def summarise(index, carry):
+    def summarise(index):
         tile = pl.ds(pl.multiple_of(index * TILE, TILE), TILE)
-        own = jnp.dot(input_ref[...], x_ref[:, tile], preferred_element_type=jnp.float32)
+        own = None
+        for rows in group_rows:
+            wide = jnp.dot(leave_ref[rows], spread_ref[:, tile], preferred_element_type=jnp.float32)
+            carried = (x_ref[rows, tile].astype(jnp.float32) * wide).astype(jnp.bfloat16)
+            part = jnp.dot(input_ref[:, rows], carried, preferred_element_type=jnp.float32)
+            own = part if own is None else own + part
         own_ref[index] = own
         own_send_ref[index] = own.astype(jnp.bfloat16)
         twin_copy(index).start()
-        return carry
-
-    lax.fori_loop(0, slices, summarise, 0)
+
+    for group in range(groups):
+        read_frames(group).wait()
 
     @pl.when(jnp.logical_not(has_prior))
     def _():
         prior_ref[...] = jnp.zeros_like(prior_ref)
 
     causal = lower_matrix(CHUNK)
-    chunks = frame_count // CHUNK
-
-    def couple(chunk, carry):
+    half = CHUNK // 2
+    batch = 2 if groups % 2 == 0 else 1
+
+    def couple_chunk(chunk, first_chunk):
         frames_here = pl.ds(pl.multiple_of(chunk * CHUNK, CHUNK), CHUNK)
         output_rows = whole_ref[head_pairs:, :, frames_here].reshape(STATE, CHUNK)
         output_map = output_rows.astype(jnp.float32).T.astype(jnp.bfloat16)
@@ -286,11 +259,30 @@
         left_ref[chunk, :CHUNK, CHUNK:] = output_map
         left_ref[chunk, CHUNK:, :CHUNK] = input_map
         left_ref[chunk, CHUNK:, CHUNK:] = jnp.zeros((STATE, STATE), jnp.bfloat16)
+        here = running_ref[frames_here]
+        middle = here[half - 1 : half]
+        last = here[CHUNK - 1 :]
+        if first_chunk:
+            before = jnp.zeros_like(last)
+        else:
+            eight = pl.ds(pl.multiple_of(chunk * CHUNK - 8, 8), 8)
+            before = running_ref[eight][7:]
+        extra = lax.broadcasted_iota(jnp.int32, (8, LANES), 0)
+        decay_ref[chunk, :CHUNK] = jnp.exp(middle - here)
+        decay_ref[chunk, CHUNK : 2 * CHUNK] = jnp.exp(here - middle)
+        decay_ref[chunk, 2 * CHUNK :] = jnp.exp(
+            jnp.where(extra == 0, middle - before, last - middle)
+        )
+
+    def couple(index, carry):
+        each = GROUP // CHUNK
+        for place in range(batch * each):
+            couple_chunk(index * (batch * each) + place, place % each == 0)
         return carry
 
     first_side = shard_side == 0
 
-    def hand_on(index, carry):
+    def hand_on(index):
         tile = pl.ds(pl.multiple_of(index * TILE, TILE), TILE)
         own_rate = rates_ref[0:1, tile]
         twin_rate = rates_ref[8:9, tile]
@@ -313,10 +305,29 @@
         enter_ref[:, tile] = jnp.where(first_side, prior, twin_rate * prior + twin).astype(
             jnp.bfloat16
         )
-        lax.fori_loop(chunks * index // slices, chunks * (index + 1) // slices, couple, 0)
+
+    lag = jnp.where(has_next, jnp.minimum(2 + 2 * shard_pair, slices), slices)
+
+    def advance(step, carry):
+        @pl.when(step < slices)
+        def _():
+            summarise(step)
+
+        @pl.when((step == slices - 1) & jnp.logical_not(has_next))
+        def _():
+            lax.fori_loop(0, groups // batch, couple, 0)
+
+        @pl.when(step >= lag)
+        def _():
+            hand_on(step - lag)
+
         return carry
 
-    lax.fori_loop(0, slices, hand_on, 0)
+    lax.fori_loop(0, slices + lag, advance, 0)
+
+    @pl.when(has_next)
+    def _():
+        lax.fori_loop(0, groups // batch, couple, 0)
 
     def finish(index, carry):
         twin_copy(index).wait_send()
@@ -354,7 +365,7 @@
             pltpu.VMEM((frame_count, columns), jnp.bfloat16),
             pltpu.VMEM((head_count,) + state_proj.shape, jnp.bfloat16),
             pltpu.VMEM((frame_count, LANES), jnp.float32),
-            pltpu.VMEM((groups, 1, LANES), jnp.float32),
+            pltpu.VMEM((frame_count, LANES), jnp.bfloat16),
             pltpu.VMEM((LANES, columns), jnp.bfloat16),
             pltpu.VMEM((slices, STATE, TILE), jnp.float32),
             pltpu.VMEM((slices, STATE, TILE), jnp.bfloat16),

time: 67.6 us -> 68.2 us (level)
  no operation moved by 1% of the time
where the time goes in v4:
time: 68.2 us; the launch traced here: 67.9 us
  Pallas kernels  63.5 us (93%)
  local copies, waits for them, and re-layouts  2.8 us (4%)
  other arithmetic  1.55 us (2%)
    pallas_call x1, Pallas kernels, enter_states(): pl.pallas_call(functools.partial(enter_kernel, shard_count, head_count),...  38.9 us
    pallas_call x1, Pallas kernels, mix(): pl.pallas_call(mix_kernel, grid_spec=grid_spec, out_shape=jax.ShapeDtypeS...  24.6 us
    unnamed x4, local copies, waits for them, and re-layouts  1.99 us

profile of v4, /device:TPU:24, one launch (start us, length us, event | category | flops | bytes accessed | tf_op | source)
XLA Modules:
  0.0 67.9 jit_solution(9062409991354981572)
XLA Ops:
  0.0 0.7 broadcast_subtract_fusion
  0.7 0.1 select_reduce_fusion.slot_ref
  0.7 0.8 %compare_convert_fusion.onward_ref = f32[12,12]{1,0:T(8,128)S(1)} fusion(s32[12]{0:T(128)} %param.9), kind=kLoop, calls=%fused_computation.2 | loop fusion | flops 288 | bytes 624 | tf_op jit(solution)/shard_map/convert_element_type | solution.py:461
  1.5 0.7 %broadcast_in_dim.22 = f32[32,64]{1,0:T(8,128)S(1)} broadcast(f32[32]{0:T(128)} %param.8), dimensions={0} | broadcast | bytes 8320 | tf_op jit(solution)/shard_map/broadcast_in_dim | solution.py:465
  2.3 0.1 broadcast_in_dim_reshape.3.skip_ref
  2.4 0.0 copy-start
  2.4 1.0 %copy-done = bf16[64,3072]{1,0:T(8,128)(2,1)S(1)} copy-done((bf16[64,3072]{1,0:T(8,128)(2,1)S(1)}, bf16[64,3072]{1,0:T(8,128)(2,1)}, u32[]{:S(2)}) %copy-start) | copy-done | bytes 393240
  3.4 0.0 copy-start.1
  3.4 1.0 %copy-done.1 = f32[32,3072]{1,0:T(8,128)S(1)} copy-done((f32[32,3072]{1,0:T(8,128)S(1)}, f32[32,3072]{1,0:T(8,128)}, u32[]{:S(2)}) %copy-start.1) | copy-done | bytes 393240
  4.4 38.9 %enter.1 = (bf16[128,2048]{1,0:T(8,128)(2,1)S(1)}, bf16[24,256,256]{2,1,0:T(8,128)(2,1)S(1)}, f32[24,264,128]{2,1,0:T(8,128)}) custom-call(bf16[3072,2048]{1,0:T(8,128)(2,1)} %x_ref.1, bf16[64,3072]{1,0:T(8,128)(2,1)S(1)} %copy-done, f32[32,3072]{1,0:T(8,128)S(1)} %copy-done.1, f32[12,12]{1,0:T(8,128)S(1)} %compare_convert_fusion.onward_ref), custom_call_target="tpu_custom_call" | custom-call | flops 3221225472 | bytes 12582912 | tf_op jit(solution)/shard_map/enter/pallas_call | solution.py:354
  43.3 24.6 %mix.1 = bf16[3072,2048]{1,0:T(8,128)(2,1)} custom-call(s32[12]{0:T(128)S(1)} %select_reduce_fusion.slot_ref, bf16[3072,2048]{1,0:T(8,128)(2,1)} %x_ref.1, bf16[24,256,256]{2,1,0:T(8,128)(2,1)S(1)} %get-tuple-element.8.left_ref, f32[24,264,128]{2,1,0:T(8,128)} %get-tuple-element.9.decay_ref, f32[1,2048]{1,0:T(1,128)S(1)} %broadcast_in_dim_reshape.3.skip_ref, ...), custom_call_target="tpu_custom_call" | custom-call | flops 6442450944 | bytes 25165824 | tf_op jit(solution)/shard_map/mix/pallas_call | solution.py:442
Async XLA Ops:
  2.4 1.0 %copy-start = (bf16[64,3072]{1,0:T(8,128)(2,1)S(1)}, bf16[64,3072]{1,0:T(8,128)(2,1)}, u32[]{:S(2)}) copy-start(bf16[64,3072]{1,0:T(8,128)(2,1)} %proj_ref.1) | copy-start | bytes 1179652
  3.4 1.0 %copy-start.1 = (f32[32,3072]{1,0:T(8,128)S(1)}, f32[32,3072]{1,0:T(8,128)}, u32[]{:S(2)}) copy-start(f32[32,3072]{1,0:T(8,128)} %log_ref.1) | copy-start | bytes 1179652

commit v5 on v4

--- a/solution.py
+++ b/solution.py
@@ -14,7 +14,6 @@
 TILE = 256
 PIECES = 2
 LANES = 128
-DECAY_ROWS = 2 * CHUNK + 8
 MESH = pl.DeviceIdType.MESH
 VMEM_BYTES = 48 * 1024 * 1024
 
@@ -24,15 +23,6 @@
     owner = lax.broadcasted_iota(jnp.int32, (LANES, columns), 1) // HEAD_DIM
     same = (rows % heads == owner) & (rows < 2 * heads)
     return same.astype(jnp.float32).astype(jnp.bfloat16)
-
-
-def widen(values, start):
-    first = lax.broadcasted_iota(jnp.int32, values.shape, 1) // HEAD_DIM
-    parts = [
-        jnp.take_along_axis(values, first + at // HEAD_DIM, axis=1, mode="promise_in_bounds")
-        for at in range(start, start + TILE, LANES)
-    ]
-    return jnp.concatenate(parts, axis=1)
 
 
 def lower_matrix(length):
@@ -248,36 +238,41 @@
     causal = lower_matrix(CHUNK)
     half = CHUNK // 2
     batch = 2 if groups % 2 == 0 else 1
-
-    def couple_chunk(chunk, first_chunk):
+    causal_terms = causal.astype(jnp.float32).astype(jnp.bfloat16)
+    frame_ids = lax.broadcasted_iota(jnp.int32, (CHUNK, CHUNK), 1)
+    onto = lax.broadcasted_iota(jnp.int32, (CHUNK, CHUNK), 0) <= frame_ids
+
+    def couple_chunk(chunk):
         frames_here = pl.ds(pl.multiple_of(chunk * CHUNK, CHUNK), CHUNK)
-        output_rows = whole_ref[head_pairs:, :, frames_here].reshape(STATE, CHUNK)
-        output_map = output_rows.astype(jnp.float32).T.astype(jnp.bfloat16)
-        input_map = input_ref[:, frames_here]
-        coupling = jnp.dot(output_map, input_map, preferred_element_type=jnp.float32)
-        left_ref[chunk, :CHUNK, :CHUNK] = jnp.where(causal, coupling, 0.0).astype(jnp.bfloat16)
-        left_ref[chunk, :CHUNK, CHUNK:] = output_map
-        left_ref[chunk, CHUNK:, :CHUNK] = input_map
+        output_map = whole_ref[head_pairs:, :, frames_here].reshape(STATE, CHUNK)
+        input_map = input_ref[:, frames_here].astype(jnp.float32).T.astype(jnp.bfloat16)
+        coupling = jnp.dot(input_map, output_map, preferred_element_type=jnp.float32)
+        left_ref[chunk, :CHUNK, :CHUNK] = jnp.where(onto, coupling, 0.0).astype(jnp.bfloat16)
+        left_ref[chunk, :CHUNK, CHUNK:] = input_map
+        left_ref[chunk, CHUNK:, :CHUNK] = output_map
         left_ref[chunk, CHUNK:, CHUNK:] = jnp.zeros((STATE, STATE), jnp.bfloat16)
-        here = running_ref[frames_here]
-        middle = here[half - 1 : half]
-        last = here[CHUNK - 1 :]
-        if first_chunk:
-            before = jnp.zeros_like(last)
-        else:
-            eight = pl.ds(pl.multiple_of(chunk * CHUNK - 8, 8), 8)
-            before = running_ref[eight][7:]
-        extra = lax.broadcasted_iota(jnp.int32, (8, LANES), 0)
-        decay_ref[chunk, :CHUNK] = jnp.exp(middle - here)
-        decay_ref[chunk, CHUNK : 2 * CHUNK] = jnp.exp(here - middle)
-        decay_ref[chunk, 2 * CHUNK :] = jnp.exp(
-            jnp.where(extra == 0, middle - before, last - middle)
-        )
+        logs = log_ref[:, frames_here]
+        high = logs.astype(jnp.bfloat16)
+        rest = logs - high.astype(jnp.float32)
+        nearer = rest.astype(jnp.bfloat16)
+        low = (rest - nearer.astype(jnp.float32)).astype(jnp.bfloat16)
+        here = None
+        for term in (low, nearer, high):
+            part = lax.dot_general(
+                term, causal_terms, (((1,), (1,)), ((), ())), preferred_element_type=jnp.float32
+            )
+            here = part if here is None else here + part
+        middle = here[:, half - 1 : half]
+        last = here[:, CHUNK - 1 :]
+        decay_ref[chunk, :heads] = jnp.exp(middle - here)
+        decay_ref[chunk, heads : 2 * heads] = jnp.exp(here - middle)
+        decay_ref[chunk, 2 * heads : 3 * heads] = jnp.exp(jnp.broadcast_to(middle, here.shape))
+        decay_ref[chunk, 3 * heads :] = jnp.exp(jnp.broadcast_to(last - middle, here.shape))
 
     def couple(index, carry):
         each = GROUP // CHUNK
         for place in range(batch * each):
-            couple_chunk(index * (batch * each) + place, place % each == 0)
+            couple_chunk(index * (batch * each) + place)
         return carry
 
     first_side = shard_side == 0
@@ -358,7 +353,7 @@
         out_shape=[
             jax.ShapeDtypeStruct((STATE, columns), jnp.bfloat16),
             jax.ShapeDtypeStruct((chunks, CHUNK + STATE, CHUNK + STATE), jnp.bfloat16),
-            jax.ShapeDtypeStruct((chunks, DECAY_ROWS, LANES), jnp.float32),
+            jax.ShapeDtypeStruct((chunks, 4 * heads, CHUNK), jnp.float32),
         ],
         scratch_shapes=[
             pltpu.VMEM((STATE, frame_count), jnp.bfloat16),
@@ -399,24 +394,38 @@
 def mix_kernel(slot_ref, x_ref, left_ref, decay_ref, skip_ref, enter_ref, out_ref, state_ref):
     step = pl.program_id(0)
     columns = x_ref.shape[1]
+    heads = columns // HEAD_DIM
 
     @pl.when(step == 0)
     def _():
-        state_ref[...] = enter_ref[...].astype(jnp.float32)
+        for start in range(0, columns, TILE):
+            tile = slice(start, start + TILE)
+            state_ref[tile] = enter_ref[:, tile].astype(jnp.float32).T
 
     for chunk in range(GROUP // CHUNK):
         rows = slice(chunk * CHUNK, (chunk + 1) * CHUNK)
         for start in range(0, columns, TILE):
             tile = slice(start, start + TILE)
-            x = x_ref[rows, tile].astype(jnp.float32)
-            scaled = x * widen(decay_ref[chunk, :CHUNK], start)
-            ends = widen(decay_ref[chunk, 2 * CHUNK :], start)
-            prior = state_ref[:, tile] * ends[0:1]
-            both = jnp.concatenate([scaled.astype(jnp.bfloat16), prior.astype(jnp.bfloat16)], axis=0)
-            sums = jnp.dot(left_ref[chunk], both, preferred_element_type=jnp.float32)
-            mixed = sums[:CHUNK] * widen(decay_ref[chunk, CHUNK : 2 * CHUNK], start)
-            out_ref[rows, tile] = (mixed + skip_ref[:, tile] * x).astype(out_ref.dtype)
-            state_ref[:, tile] = (prior + sums[CHUNK:]) * ends[1:2]
+            heads_here = range(start // HEAD_DIM, (start + TILE) // HEAD_DIM)
+
+            def spread(ref, first):
+                return jnp.concatenate(
+                    [
+                        jnp.broadcast_to(ref[first + head : first + head + 1], (HEAD_DIM, CHUNK))
+                        for head in heads_here
+                    ],
+                    axis=0,
+                )
+
+            factors = decay_ref.at[chunk]
+            x = x_ref[rows, tile].T.astype(jnp.float32)
+            scaled = x * spread(factors, 0)
+            prior = state_ref[tile] * spread(factors, 2 * heads)
+            both = jnp.concatenate([scaled.astype(jnp.bfloat16), prior.astype(jnp.bfloat16)], axis=1)
+            sums = jnp.dot(both, left_ref[chunk], preferred_element_type=jnp.float32)
+            mixed = sums[:, :CHUNK] * spread(factors, heads) + spread(skip_ref, 0) * x
+            out_ref[rows, tile] = mixed.astype(out_ref.dtype).T
+            state_ref[tile] = (prior + sums[:, CHUNK:]) * spread(factors, 3 * heads)
 
 
 def mix(slots, frames, left, decay, skip, entering):
@@ -431,13 +440,11 @@
             pl.BlockSpec((GROUP, columns), lambda i, slot: (slot[i], 0)),
             pl.BlockSpec((each,) + left.shape[1:], lambda i, slot: (slot[i], 0, 0)),
             pl.BlockSpec((each,) + decay.shape[1:], lambda i, slot: (slot[i], 0, 0)),
-            pl.BlockSpec((1, columns), lambda i, slot: (0, 0)),
+            pl.BlockSpec((heads, CHUNK), lambda i, slot: (0, 0)),
             pl.BlockSpec((STATE, columns), lambda i, slot: (0, 0)),
         ],
         out_specs=pl.BlockSpec((GROUP, columns), lambda i, slot: (i, 0)),
-        scratch_shapes=[
-            pltpu.VMEM((STATE, columns), jnp.float32),
-        ],
+        scratch_shapes=[pltpu.VMEM((columns, STATE), jnp.float32)],
     )
     return pl.pallas_call(
         mix_kernel,
@@ -462,7 +469,7 @@
     entering, left, decay = enter_states(
         shard_count, head_count, frames, state_proj, log_decay, onward
     )
-    skip = jnp.repeat(skip_gain, HEAD_DIM)[None]
+    skip = jnp.broadcast_to(skip_gain[:, None], (skip_gain.shape[0], CHUNK))
     return mix(slots, frames, left, decay, skip, entering)
 
 

time: 68.2 us -> 63.2 us (0.927)
  the two profiles are of different devices: /device:TPU:24 before, /device:TPU:16 now
where the time goes in v5:
time: 63.2 us; the launch traced here: 62.6 us
  Pallas kernels  58.3 us (92%)
  local copies, waits for them, and re-layouts  2.72 us (4%)
  other arithmetic  1.55 us (2%)
    pallas_call x1, Pallas kernels, enter_states(): pl.pallas_call(functools.partial(enter_kernel, shard_count, head_count),...  38.1 us
    pallas_call x1, Pallas kernels, mix(): pl.pallas_call(mix_kernel, grid_spec=grid_spec, out_shape=jax.ShapeDtypeS...  20.2 us
    unnamed x4, local copies, waits for them, and re-layouts  1.99 us

profile of v5, /device:TPU:16, one launch (start us, length us, event | category | flops | bytes accessed | tf_op | source)
XLA Modules:
  0.0 62.6 jit_solution(3373021834448389325)
XLA Ops:
  0.0 0.7 %broadcast_subtract_fusion = s32[12]{0:T(128)S(1)} fusion(s32[12]{0:T(128)} %param.9, s32[]{:T(128)S(6)} %mul.3), kind=kLoop, calls=%fused_computation.3 | loop fusion | flops 12 | bytes 100 | tf_op jit(solution)/shard_map/sub | solution.py:465
  0.7 0.1 select_reduce_fusion.slot_ref
  0.7 0.8 %compare_convert_fusion.onward_ref = f32[12,12]{1,0:T(8,128)S(1)} fusion(s32[12]{0:T(128)} %param.9), kind=kLoop, calls=%fused_computation.2 | loop fusion | flops 288 | bytes 624 | tf_op jit(solution)/shard_map/convert_element_type | solution.py:468
  1.5 0.7 %broadcast_in_dim.16.skip_ref = f32[32,128]{1,0:T(8,128)S(1)} broadcast(f32[32]{0:T(128)} %param.8), dimensions={0} | broadcast | bytes 16512 | tf_op jit(solution)/shard_map/broadcast_in_dim | solution.py:472
  2.3 0.0 copy-start
  2.3 1.0 %copy-done = bf16[64,3072]{1,0:T(8,128)(2,1)S(1)} copy-done((bf16[64,3072]{1,0:T(8,128)(2,1)S(1)}, bf16[64,3072]{1,0:T(8,128)(2,1)}, u32[]{:S(2)}) %copy-start) | copy-done | bytes 393240
  3.3 0.0 copy-start.1
  3.3 1.0 %copy-done.1 = f32[32,3072]{1,0:T(8,128)S(1)} copy-done((f32[32,3072]{1,0:T(8,128)S(1)}, f32[32,3072]{1,0:T(8,128)}, u32[]{:S(2)}) %copy-start.1) | copy-done | bytes 393240
  4.3 38.1 %enter.1 = (bf16[128,2048]{1,0:T(8,128)(2,1)S(1)}, bf16[24,256,256]{2,1,0:T(8,128)(2,1)S(1)}, f32[24,128,128]{2,1,0:T(8,128)S(1)}) custom-call(bf16[3072,2048]{1,0:T(8,128)(2,1)} %x_ref.1, bf16[64,3072]{1,0:T(8,128)(2,1)S(1)} %copy-done, f32[32,3072]{1,0:T(8,128)S(1)} %copy-done.1, f32[12,12]{1,0:T(8,128)S(1)} %compare_convert_fusion.onward_ref), custom_call_target="tpu_custom_call" | custom-call | flops 3221225472 | bytes 12582912 | tf_op jit(solution)/shard_map/enter/pallas_call | solution.py:349
  42.4 20.2 %mix.1 = bf16[3072,2048]{1,0:T(8,128)(2,1)} custom-call(s32[12]{0:T(128)S(1)} %select_reduce_fusion.slot_ref, bf16[3072,2048]{1,0:T(8,128)(2,1)} %x_ref.1, bf16[24,256,256]{2,1,0:T(8,128)(2,1)S(1)} %get-tuple-element.8.left_ref, f32[24,128,128]{2,1,0:T(8,128)S(1)} %get-tuple-element.9.decay_ref, f32[32,128]{1,0:T(8,128)S(1)} %broadcast_in_dim.16.skip_ref, ...), custom_call_target="tpu_custom_call" | custom-call | flops 6442450944 | bytes 25165824 | tf_op jit(solution)/shard_map/mix/pallas_call | solution.py:449
Async XLA Ops:
  2.3 1.0 %copy-start = (bf16[64,3072]{1,0:T(8,128)(2,1)S(1)}, bf16[64,3072]{1,0:T(8,128)(2,1)}, u32[]{:S(2)}) copy-start(bf16[64,3072]{1,0:T(8,128)(2,1)} %proj_ref.1) | copy-start | bytes 1179652
  3.3 1.0 %copy-start.1 = (f32[32,3072]{1,0:T(8,128)S(1)}, f32[32,3072]{1,0:T(8,128)}, u32[]{:S(2)}) copy-start(f32[32,3072]{1,0:T(8,128)} %log_ref.1) | copy-start | bytes 1179652

commit v6 on v5

--- a/solution.py
+++ b/solution.py
@@ -18,13 +18,6 @@
 VMEM_BYTES = 48 * 1024 * 1024
 
 
-def spread_matrix(heads, columns):
-    rows = lax.broadcasted_iota(jnp.int32, (LANES, columns), 0)
-    owner = lax.broadcasted_iota(jnp.int32, (LANES, columns), 1) // HEAD_DIM
-    same = (rows % heads == owner) & (rows < 2 * heads)
-    return same.astype(jnp.float32).astype(jnp.bfloat16)
-
-
 def lower_matrix(length):
     rows = lax.broadcasted_iota(jnp.int32, (length, length), 0)
     columns = lax.broadcasted_iota(jnp.int32, (length, length), 1)
@@ -45,10 +38,18 @@
     return total
 
 
-def two_terms(values, heads):
-    high = values.astype(jnp.bfloat16).astype(jnp.float32)
-    lanes = lax.broadcasted_iota(jnp.int32, values.shape, 1)
-    return jnp.where(lanes < heads, high, values - high).astype(jnp.bfloat16)
+def row_sums(logs, lower):
+    high = logs.astype(jnp.bfloat16)
+    rest = logs - high.astype(jnp.float32)
+    middle = rest.astype(jnp.bfloat16)
+    low = (rest - middle.astype(jnp.float32)).astype(jnp.bfloat16)
+    total = None
+    for term in (low, middle, high):
+        part = lax.dot_general(
+            term, lower, (((1,), (1,)), ((), ())), preferred_element_type=jnp.float32
+        )
+        total = part if total is None else total + part
+    return total
 
 
 def enter_kernel(
@@ -64,9 +65,8 @@
     input_ref,
     x_ref,
     whole_ref,
-    running_ref,
     leave_ref,
-    spread_ref,
+    turned_ref,
     own_ref,
     own_send_ref,
     twin_ref,
@@ -151,16 +151,18 @@
         proj_copies[-1].start()
     whole_ref[head] = proj_ref[...]
 
-    spread_ref[...] = spread_matrix(heads, columns)
     lower = lower_matrix(GROUP).astype(jnp.float32).astype(jnp.bfloat16)
-
+    ones = jnp.ones((8, GROUP), jnp.bfloat16)
     group_rows = [slice(group * GROUP, (group + 1) * GROUP) for group in range(groups)]
-    for rows in group_rows:
-        logs = log_ref[:, rows]
-        running_ref[rows] = select_sums(lower, jnp.concatenate([logs] * (LANES // heads), axis=0), 1)
-    group_logs = jnp.concatenate([running_ref[rows.stop - 1 : rows.stop] for rows in group_rows], axis=0)
-    total = jnp.sum(group_logs, axis=0, keepdims=True)
-    total_ref[...] = jnp.broadcast_to(total, total_ref.shape)
+    group_logs = jnp.concatenate(
+        [
+            select_sums(ones, jnp.concatenate([log_ref[:, rows]] * (LANES // heads), axis=0), 1)[:1]
+            for rows in group_rows
+        ],
+        axis=0,
+    )
+    after = select_sums(onward_ref[...].astype(jnp.bfloat16), group_logs, 0).T
+    total_ref[...] = jnp.broadcast_to(after[:heads, groups : groups + 1], total_ref.shape)
     total_copy = pltpu.make_async_remote_copy(
         src_ref=total_ref,
         dst_ref=twin_total_ref,
@@ -170,10 +172,9 @@
         device_id_type=MESH,
     )
     total_copy.start()
-    after = select_sums(onward_ref[...].astype(jnp.bfloat16), group_logs, 0)
     for group, rows in enumerate(group_rows):
-        leaving = jnp.exp(after[group : group + 1] - running_ref[rows])
-        leave_ref[rows] = two_terms(leaving, heads)
+        running = row_sums(log_ref[:, rows], lower)
+        leave_ref[:, rows] = jnp.exp(after[:heads, group : group + 1] - running)
 
     for part in range(PIECES):
         for away in range(1, head_pairs):
@@ -191,10 +192,20 @@
         input_ref[owner * rows_each : (owner + 1) * rows_each] = whole_ref[owner]
 
     total_copy.wait()
-    both_totals = jnp.concatenate([total_ref[...], twin_total_ref[...]], axis=0)
-    rates_ref[...] = jnp.dot(
-        two_terms(jnp.exp(both_totals), heads), spread_ref[...], preferred_element_type=jnp.float32
-    )
+    rates_ref[:heads] = jnp.exp(total_ref[...])
+    rates_ref[heads:] = jnp.exp(twin_total_ref[...])
+    for rows in group_rows:
+        turned_ref[rows] = input_ref[:, rows].astype(jnp.float32).T.astype(jnp.bfloat16)
+    heads_each = TILE // HEAD_DIM
+
+    def spread(ref, first, lanes):
+        return jnp.concatenate(
+            [
+                jnp.broadcast_to(ref[pl.ds(first + head, 1), lanes], (HEAD_DIM, lanes.stop - lanes.start))
+                for head in range(heads_each)
+            ],
+            axis=0,
+        )
 
     def twin_copy(index):
         return pltpu.make_async_remote_copy(
@@ -220,9 +231,9 @@
         tile = pl.ds(pl.multiple_of(index * TILE, TILE), TILE)
         own = None
         for rows in group_rows:
-            wide = jnp.dot(leave_ref[rows], spread_ref[:, tile], preferred_element_type=jnp.float32)
-            carried = (x_ref[rows, tile].astype(jnp.float32) * wide).astype(jnp.bfloat16)
-            part = jnp.dot(input_ref[:, rows], carried, preferred_element_type=jnp.float32)
+            wide = spread(leave_ref, index * heads_each, rows)
+            carried = (x_ref[rows, tile].T.astype(jnp.float32) * wide).astype(jnp.bfloat16)
+            part = jnp.dot(carried, turned_ref[rows], preferred_element_type=jnp.float32)
             own = part if own is None else own + part
         own_ref[index] = own
         own_send_ref[index] = own.astype(jnp.bfloat16)
@@ -252,16 +263,7 @@
         left_ref[chunk, CHUNK:, :CHUNK] = output_map
         left_ref[chunk, CHUNK:, CHUNK:] = jnp.zeros((STATE, STATE), jnp.bfloat16)
         logs = log_ref[:, frames_here]
-        high = logs.astype(jnp.bfloat16)
-        rest = logs - high.astype(jnp.float32)
-        nearer = rest.astype(jnp.bfloat16)
-        low = (rest - nearer.astype(jnp.float32)).astype(jnp.bfloat16)
-        here = None
-        for term in (low, nearer, high):
-            part = lax.dot_general(
-                term, causal_terms, (((1,), (1,)), ((), ())), preferred_element_type=jnp.float32
-            )
-            here = part if here is None else here + part
+        here = row_sums(logs, causal_terms)
         middle = here[:, half - 1 : half]
         last = here[:, CHUNK - 1 :]
         decay_ref[chunk, :heads] = jnp.exp(middle - here)
@@ -279,8 +281,8 @@
 
     def hand_on(index):
         tile = pl.ds(pl.multiple_of(index * TILE, TILE), TILE)
-        own_rate = rates_ref[0:1, tile]
-        twin_rate = rates_ref[8:9, tile]
+        own_rate = spread(rates_ref, index * heads_each, slice(0, STATE))
+        twin_rate = spread(rates_ref, heads + index * heads_each, slice(0, STATE))
         twin_copy(index).wait_recv()
 
         @pl.when(has_prior)
@@ -297,7 +299,7 @@
             next_ref[index] = (own_rate * twin_rate * prior + pair_sum).astype(jnp.bfloat16)
             next_copy(index).start()
 
-        enter_ref[:, tile] = jnp.where(first_side, prior, twin_rate * prior + twin).astype(
+        enter_ref[tile] = jnp.where(first_side, prior, twin_rate * prior + twin).astype(
             jnp.bfloat16
         )
 
@@ -351,7 +353,7 @@
         in_specs=[pl.BlockSpec(memory_space=pl.ANY), vmem, vmem, vmem],
         out_specs=[vmem] * 3,
         out_shape=[
-            jax.ShapeDtypeStruct((STATE, columns), jnp.bfloat16),
+            jax.ShapeDtypeStruct((columns, STATE), jnp.bfloat16),
             jax.ShapeDtypeStruct((chunks, CHUNK + STATE, CHUNK + STATE), jnp.bfloat16),
             jax.ShapeDtypeStruct((chunks, 4 * heads, CHUNK), jnp.float32),
         ],
@@ -359,17 +361,16 @@
             pltpu.VMEM((STATE, frame_count), jnp.bfloat16),
             pltpu.VMEM((frame_count, columns), jnp.bfloat16),
             pltpu.VMEM((head_count,) + state_proj.shape, jnp.bfloat16),
-            pltpu.VMEM((frame_count, LANES), jnp.float32),
-            pltpu.VMEM((frame_count, LANES), jnp.bfloat16),
-            pltpu.VMEM((LANES, columns), jnp.bfloat16),
-            pltpu.VMEM((slices, STATE, TILE), jnp.float32),
-            pltpu.VMEM((slices, STATE, TILE), jnp.bfloat16),
-            pltpu.VMEM((slices, STATE, TILE), jnp.bfloat16),
-            pltpu.VMEM((slices, STATE, TILE), jnp.bfloat16),
-            pltpu.VMEM((slices, STATE, TILE), jnp.bfloat16),
-            pltpu.VMEM((8, 128), jnp.float32),
-            pltpu.VMEM((8, 128), jnp.float32),
-            pltpu.VMEM((16, columns), jnp.float32),
+            pltpu.VMEM((heads, frame_count), jnp.float32),
+            pltpu.VMEM((frame_count, STATE), jnp.bfloat16),
+            pltpu.VMEM((slices, TILE, STATE), jnp.float32),
+            pltpu.VMEM((slices, TILE, STATE), jnp.bfloat16),
+            pltpu.VMEM((slices, TILE, STATE), jnp.bfloat16),
+            pltpu.VMEM((slices, TILE, STATE), jnp.bfloat16),
+            pltpu.VMEM((slices, TILE, STATE), jnp.bfloat16),
+            pltpu.VMEM((heads, STATE), jnp.float32),
+            pltpu.VMEM((heads, STATE), jnp.float32),
+            pltpu.VMEM((2 * heads, STATE), jnp.float32),
             dma((groups,)),
             dma((head_count, PIECES)),
             dma((head_count, PIECES)),
@@ -398,9 +399,7 @@
 
     @pl.when(step == 0)
     def _():
-        for start in range(0, columns, TILE):
-            tile = slice(start, start + TILE)
-            state_ref[tile] = enter_ref[:, tile].astype(jnp.float32).T
+        state_ref[...] = enter_ref[...].astype(jnp.float32)
 
     for chunk in range(GROUP // CHUNK):
         rows = slice(chunk * CHUNK, (chunk + 1) * CHUNK)
@@ -441,7 +440,7 @@
             pl.BlockSpec((each,) + left.shape[1:], lambda i, slot: (slot[i], 0, 0)),
             pl.BlockSpec((each,) + decay.shape[1:], lambda i, slot: (slot[i], 0, 0)),
             pl.BlockSpec((heads, CHUNK), lambda i, slot: (0, 0)),
-            pl.BlockSpec((STATE, columns), lambda i, slot: (0, 0)),
+            pl.BlockSpec((columns, STATE), lambda i, slot: (0, 0)),
         ],
         out_specs=pl.BlockSpec((GROUP, columns), lambda i, slot: (i, 0)),
         scratch_shapes=[pltpu.VMEM((columns, STATE), jnp.float32)],
@@ -465,7 +464,8 @@
     place = group_pos - lax.axis_index("seq") * groups
     slot_ids = jnp.arange(groups, dtype=jnp.int32)
     slots = jnp.sum(jnp.where(place[:, None] == slot_ids[None, :], slot_ids[:, None], 0), axis=0)
-    onward = (group_pos[None, :] >= group_pos[:, None]).astype(jnp.float32)
+    floor = jnp.concatenate([group_pos, jnp.zeros((1,), group_pos.dtype)])
+    onward = (group_pos[None, :] >= floor[:, None]).astype(jnp.float32)
     entering, left, decay = enter_states(
         shard_count, head_count, frames, state_proj, log_decay, onward
     )

time: 63.2 us -> 63.1 us (level)
  the two profiles are of different devices: /device:TPU:16 before, /device:TPU:24 now
where the time goes in v6:
time: 63.1 us; the launch traced here: 61.9 us
  Pallas kernels  57 us (90%)
  local copies, waits for them, and re-layouts  2.72 us (4%)
  other arithmetic  2.2 us (3%)
    pallas_call x1, Pallas kernels, enter_states(): pl.pallas_call(functools.partial(enter_kernel, shard_count, head_count),...  37 us
    pallas_call x1, Pallas kernels, mix(): pl.pallas_call(mix_kernel, grid_spec=grid_spec, out_shape=jax.ShapeDtypeS...  20 us
    unnamed x4, local copies, waits for them, and re-layouts  1.99 us

profile of v6, /device:TPU:24, one launch (start us, length us, event | category | flops | bytes accessed | tf_op | source)
XLA Modules:
  0.0 61.9 jit_solution(817425790554815526)
XLA Ops:
  0.0 0.7 %broadcast_subtract_fusion = s32[12]{0:T(128)S(1)} fusion(s32[12]{0:T(128)} %param.9, s32[]{:T(128)S(6)} %mul.3), kind=kLoop, calls=%fused_computation.4 | loop fusion | flops 12 | bytes 100 | tf_op jit(solution)/shard_map/sub | solution.py:464
  0.7 0.1 select_reduce_fusion.slot_ref
  0.7 0.7 %pad_add_fusion = s32[13]{0:T(128)S(1)} fusion(s32[1]{0:T(128)} %constant.11.clone.1, s32[12]{0:T(128)} %param.9), kind=kLoop, calls=%fused_computation.3 | loop fusion | flops 13 | bytes 104 | tf_op jit(solution)/shard_map/concatenate | solution.py:467
  1.5 0.7 %compare_convert_fusion.onward_ref = f32[13,12]{1,0:T(8,128)S(1)} fusion(s32[12]{0:T(128)} %param.9, s32[13]{0:T(128)S(1)} %pad_add_fusion), kind=kLoop, calls=%fused_computation.2 | loop fusion | flops 312 | bytes 724 | tf_op jit(solution)/shard_map/convert_element_type | solution.py:468
  2.2 0.7 %broadcast_in_dim.16.skip_ref = f32[32,128]{1,0:T(8,128)S(1)} broadcast(f32[32]{0:T(128)} %param.8), dimensions={0} | broadcast | bytes 16512 | tf_op jit(solution)/shard_map/broadcast_in_dim | solution.py:472
  2.9 0.0 copy-start
  2.9 1.0 %copy-done = bf16[64,3072]{1,0:T(8,128)(2,1)S(1)} copy-done((bf16[64,3072]{1,0:T(8,128)(2,1)S(1)}, bf16[64,3072]{1,0:T(8,128)(2,1)}, u32[]{:S(2)}) %copy-start) | copy-done | bytes 393240
  3.9 0.0 copy-start.1
  3.9 1.0 %copy-done.1 = f32[32,3072]{1,0:T(8,128)S(1)} copy-done((f32[32,3072]{1,0:T(8,128)S(1)}, f32[32,3072]{1,0:T(8,128)}, u32[]{:S(2)}) %copy-start.1) | copy-done | bytes 393240
  4.9 37.0 %enter.1 = (bf16[2048,128]{1,0:T(8,128)(2,1)S(1)}, bf16[24,256,256]{2,1,0:T(8,128)(2,1)S(1)}, f32[24,128,128]{2,1,0:T(8,128)S(1)}) custom-call(bf16[3072,2048]{1,0:T(8,128)(2,1)} %x_ref.1, bf16[64,3072]{1,0:T(8,128)(2,1)S(1)} %copy-done, f32[32,3072]{1,0:T(8,128)S(1)} %copy-done.1, f32[13,12]{1,0:T(8,128)S(1)} %compare_convert_fusion.onward_ref), custom_call_target="tpu_custom_call" | custom-call | flops 3221225472 | bytes 12582912 | tf_op jit(solution)/shard_map/enter/pallas_call | solution.py:351
  41.9 20.0 %mix.1 = bf16[3072,2048]{1,0:T(8,128)(2,1)} custom-call(s32[12]{0:T(128)S(1)} %select_reduce_fusion.slot_ref, bf16[3072,2048]{1,0:T(8,128)(2,1)} %x_ref.1, bf16[24,256,256]{2,1,0:T(8,128)(2,1)S(1)} %get-tuple-element.8.left_ref, f32[24,128,128]{2,1,0:T(8,128)S(1)} %get-tuple-element.9.decay_ref, f32[32,128]{1,0:T(8,128)S(1)} %broadcast_in_dim.16.skip_ref, ...), custom_call_target="tpu_custom_call" | custom-call | flops 6442450944 | bytes 25165824 | tf_op jit(solution)/shard_map/mix/pallas_call | solution.py:448
Async XLA Ops:
  2.9 1.0 %copy-start = (bf16[64,3072]{1,0:T(8,128)(2,1)S(1)}, bf16[64,3072]{1,0:T(8,128)(2,1)}, u32[]{:S(2)}) copy-start(bf16[64,3072]{1,0:T(8,128)(2,1)} %proj_ref.1) | copy-start | bytes 1179652
  3.9 1.0 %copy-start.1 = (f32[32,3072]{1,0:T(8,128)S(1)}, f32[32,3072]{1,0:T(8,128)}, u32[]{:S(2)}) copy-start(f32[32,3072]{1,0:T(8,128)} %log_ref.1) | copy-start | bytes 1179652
